TPU v7x, 512 devices: a whole 4x8x8 slice. The times are simulated.
512 devices in a mesh: ctx: 64 (over y, x, core), tp: 8 (over z).
Axes of the slice: x: 4, y: 8, z: 8, core: 2. Of those that a mesh axis runs over, the one named last changes fastest.
Arguments:
- q_pre: bfloat16 [16384, 5120], P('ctx', 'tp'), may hold values from -360 to 360, as said below
- k_pre: bfloat16 [16384, 5120], P('ctx', 'tp'), may hold values from -360 to 360, as said below
- values: bfloat16 [16384, 5120], P('ctx', 'tp'), may hold values from -6 to 6
- q_gain: float32 [5120], P('tp'), may hold values from 0.1 to 1.9
- k_gain: float32 [5120], P('tp'), may hold values from 0.1 to 1.9
- grad_out: bfloat16 [16384, 5120], P('ctx', 'tp'), may hold values from -6 to 6
- far_frames: int32 [64, 6], P('ctx'), may hold values from 0 to 63, as said below
- far_blocks: int32 [64, 6], P('ctx'), may hold values from 0 to 1, as said below
Outputs:
- attn_out: bfloat16 [16384, 5120], P('ctx', 'tp')
- dq_pre: bfloat16 [16384, 5120], P('ctx', 'tp')
- dk_pre: bfloat16 [16384, 5120], P('ctx', 'tp')
- dv: bfloat16 [16384, 5120], P('ctx', 'tp')
- dq_gain: float32 [5120], P('tp')
- dk_gain: float32 [5120], P('tp')
Inputs may be any that keep to these rules, and one draw needn't show every extreme that they name: far_frames[f, j] is f + 2^j or f - 2^j, the one that lies in 0 to 63 where only one does. `far_blocks`: a block index within the frame. `q_pre`: real feature values. `k_pre`: real feature values.
All inputs are finite; a program needn't handle non-finite values.
Results may differ from a plain program's by a relative error of at most 0.009.
The roundings to bfloat16 on the way count: a program that leaves them out, or rounds other values in their place, can miss the bound.
Values may be sent and summed in bfloat16 or wider, within the bound.
No kernel may reach another device: no remote copies, remote signals or barrier semaphores. Data moves between devices by JAX's collectives and lax.ppermute only.
A program may use at most 64 MiB of HBM per device.

v0:
```python
import jax
import jax.numpy as jnp
from jax import lax
from jax.sharding import PartitionSpec as P

HD = 128
BLK = 128


EPS = 1e-06


def from_behind_2(value, axis, steps):
    count = lax.axis_size(axis)
    leading, last = (max(0, -steps), min(count, count - steps))
    return lax.ppermute(value, axis, [(source, source + steps) for source in range(leading, last)])


def block_rows(matrix, block_index):
    return lax.dynamic_slice_in_dim(matrix, block_index * BLK, BLK, 0)


def add_block(total, piece, block_index):
    updated = block_rows(total, block_index) + piece.astype(jnp.float32)
    return lax.dynamic_update_slice_in_dim(total, updated, block_index * BLK, 0)


def head_major(matrix, head_count):
    return jnp.transpose(matrix.reshape(matrix.shape[0], head_count, HD), (1, 0, 2))


def row_major(stacked):
    return jnp.transpose(stacked, (1, 0, 2)).reshape(stacked.shape[1], -1)


def one_head(operands):
    queries, keys, vals, grads = operands
    softmax_scale = HD ** (-0.5)
    scores = jnp.dot(queries, keys.T, preferred_element_type=jnp.float32) * softmax_scale
    top = jnp.max(scores, axis=1, keepdims=True)
    log_total = top + jnp.log(jnp.sum(jnp.exp(scores - top), axis=1, keepdims=True))
    probs = jnp.exp(scores - log_total)
    probs_half = probs.astype(jnp.bfloat16)
    attn = jnp.dot(probs_half, vals, preferred_element_type=jnp.float32).astype(jnp.bfloat16)
    delta = jnp.sum(grads.astype(jnp.float32) * attn.astype(jnp.float32), axis=1, keepdims=True)
    dprobs = jnp.dot(grads, vals.T, preferred_element_type=jnp.float32)
    dscores = (probs * (dprobs - delta)).astype(jnp.bfloat16)
    query_grad = jnp.dot(dscores, keys, preferred_element_type=jnp.float32) * softmax_scale
    key_grad = jnp.dot(dscores.T, queries, preferred_element_type=jnp.float32) * softmax_scale
    value_grad = jnp.dot(probs_half.T, grads, preferred_element_type=jnp.float32)
    return (attn, query_grad, key_grad, value_grad)


def per_device(q_pre, k_pre, values, q_gain, k_gain, grad_out, far_frames, far_blocks):
    row_count, col_count = q_pre.shape
    head_count = col_count // HD
    width_all = col_count * lax.axis_size("tp")
    frame_count = lax.axis_size("ctx")
    band_count = frame_count.bit_length() - 1
    frame_index = lax.axis_index("ctx")
    q_float = q_pre.astype(jnp.float32)
    k_float = k_pre.astype(jnp.float32)
    q_square, k_square = lax.psum(
        (jnp.sum(q_float * q_float, axis=1), jnp.sum(k_float * k_float, axis=1)), "tp"
    )
    q_rstd = lax.rsqrt(q_square / width_all + EPS)[:, None]
    k_rstd = lax.rsqrt(k_square / width_all + EPS)[:, None]
    q_normed = (q_float * q_rstd * q_gain).astype(jnp.bfloat16)
    k_normed = (k_float * k_rstd * k_gain).astype(jnp.bfloat16)
    all_blocks = lax.all_gather(far_blocks, "ctx", axis=0, tiled=True)
    go_ahead = far_frames[0] > frame_index
    my_blocks = far_blocks[0]

    def give_back(payload, offset):
        return from_behind_2((payload[0], payload[1]), "ctx", offset)

    far_keys = []
    far_values = []
    for band_index in range(band_count):
        stride = 1 << band_index
        ahead_flag = go_ahead[band_index]
        wanted = my_blocks[band_index]

        def fetch_frame(offset):
            return from_behind_2((k_normed, values), "ctx", offset)

        from_ahead = fetch_frame(-stride)
        from_behind = fetch_frame(stride)
        far_keys.append(
            jnp.where(
                ahead_flag, block_rows(from_ahead[0], wanted), block_rows(from_behind[0], wanted)
            )
        )
        far_values.append(
            jnp.where(
                ahead_flag, block_rows(from_ahead[1], wanted), block_rows(from_behind[1], wanted)
            )
        )
    keys = head_major(jnp.concatenate([k_normed] + far_keys, axis=0), head_count)
    vals = head_major(jnp.concatenate([values] + far_values, axis=0), head_count)
    queries = head_major(q_normed, head_count)
    grads = head_major(grad_out, head_count)
    attn, query_grad, key_grad, value_grad = lax.map(one_head, (queries, keys, vals, grads))
    attn = row_major(attn)
    key_grad = row_major(key_grad)
    value_grad = row_major(value_grad)
    key_total = key_grad[:row_count]
    value_total = value_grad[:row_count]
    for band_index in range(band_count):
        stride = 1 << band_index
        ahead_flag = go_ahead[band_index]
        offset_rows = row_count + band_index * BLK
        part_key = key_grad[offset_rows : offset_rows + BLK].astype(jnp.bfloat16)
        part_value = value_grad[offset_rows : offset_rows + BLK].astype(jnp.bfloat16)
        blank = jnp.zeros_like(part_key)
        to_ahead = (
            jnp.where(ahead_flag, part_key, blank),
            jnp.where(ahead_flag, part_value, blank),
        )
        to_behind = (
            jnp.where(ahead_flag, blank, part_key),
            jnp.where(ahead_flag, blank, part_value),
        )
        from_behind = give_back(to_ahead, stride)
        from_ahead = give_back(to_behind, -stride)
        behind_reader = jnp.clip(frame_index - stride, 0, frame_count - 1)
        ahead_reader = jnp.clip(frame_index + stride, 0, frame_count - 1)
        slot_behind = all_blocks[behind_reader, band_index]
        slot_ahead = all_blocks[ahead_reader, band_index]
        key_total = add_block(
            add_block(key_total, from_behind[0], slot_behind), from_ahead[0], slot_ahead
        )
        value_total = add_block(
            add_block(value_total, from_behind[1], slot_behind), from_ahead[1], slot_ahead
        )
    q_grad_normed = row_major(query_grad)
    q_inner = jnp.sum(q_grad_normed * q_gain * q_float, axis=1)
    k_inner = jnp.sum(key_total * k_gain * k_float, axis=1)
    q_inner, k_inner = lax.psum((q_inner, k_inner), "tp")
    dq_pre = (
        q_rstd * q_gain * q_grad_normed
        - q_float * q_rstd * q_rstd * q_rstd * (q_inner / width_all)[:, None]
    ).astype(jnp.bfloat16)
    dk_pre = (
        k_rstd * k_gain * key_total
        - k_float * k_rstd * k_rstd * k_rstd * (k_inner / width_all)[:, None]
    ).astype(jnp.bfloat16)
    q_gain_grad = jnp.sum(q_grad_normed * q_float * q_rstd, axis=0)
    k_gain_grad = jnp.sum(key_total * k_float * k_rstd, axis=0)
    q_gain_grad, k_gain_grad = lax.psum((q_gain_grad, k_gain_grad), "ctx")
    return (attn, dq_pre, dk_pre, value_total.astype(jnp.bfloat16), q_gain_grad, k_gain_grad)


def solution(mesh):
    placed = (
        P("ctx", "tp"),
        P("ctx", "tp"),
        P("ctx", "tp"),
        P("tp"),
        P("tp"),
        P("ctx", "tp"),
        P("ctx", None),
        P("ctx", None),
    )
    return jax.shard_map(
        per_device,
        mesh=mesh,
        in_specs=placed,
        out_specs=(
            P("ctx", "tp"),
            P("ctx", "tp"),
            P("ctx", "tp"),
            P("ctx", "tp"),
            P("tp"),
            P("tp"),
        ),
        check_vma=False,
    )
```

profile of v0, /device:TPU:1, one launch (start us, length us, event | category | flops | bytes accessed | tf_op | source)
XLA Modules:
  0.0 587.5 jit_solution(10016206719557015080)
XLA Ops:
  3.2 20.3 %all-reduce.2 = (f32[256]{0:T(256)S(1)}, f32[256]{0:T(256)S(1)}) all-reduce(f32[256]{0:T(256)S(1)} %fusion.44, f32[256]{0:T(256)S(1)} %fusion.48), channel_id=1, replica_groups=mesh['ctx'=64,'tp'=8] {'tp'}, use_global_device_ids=true, to_apply=%region_1.0 | all-reduce | flops 512 | bytes 4096 | tf_op jit(solution)/shard_map/psum | solution.py:63
  24.4 6.3 %collective-permute-start = (bf16[256,640]{0,1:T(8,128)(2,1)S(1)}, bf16[256,640]{0,1:T(8,128)(2,1)}, u32[]{:S(2)}, u32[]{:S(2)}) collective-permute-start(bf16[256,640]{0,1:T(8,128)(2,1)S(1)} %get-tuple-element.119), channel_id=1, source_target_pairs={{8,0},{16,8},{24,16},{32,24},{40,32},{48,40},{56,48},{64,56},{72,6... | collective-permute-start | bytes 983048 | tf_op jit(solution)/shard_map/ppermute | solution.py:16
  30.8 3.0 collective-permute-start.1
  35.1 4.8 collective-permute-start.3
  46.7 40.5 %all-gather = s32[64,1,6]{2,1,0:T(1,128)S(1)} all-gather(s32[1,1,6]{2,1,0:T(1,128)S(1)} %bitcast.181), channel_id=1, replica_groups=mesh['ctx'=64,'tp'=8] {'ctx'}, dimensions={0}, use_global_device_ids=true | all-gather | bytes 1560 | tf_op jit(solution)/shard_map/all_gather | solution.py:70
  96.0 2.1 collective-permute-start.12
  98.0 3.5 collective-permute-start.13
  102.3 3.2 collective-permute-start.5
  107.6 5.4 collective-permute-start.15
  113.0 2.3 select_dynamic-update-slice_fusion.11
  116.6 4.0 collective-permute-start.7
  123.2 5.5 collective-permute-start.17
  128.7 2.3 select_dynamic-update-slice_fusion.10
  132.3 1.4 select_dynamic-update-slice_fusion.4
  135.0 4.0 collective-permute-start.19
  139.1 1.4 select_dynamic-update-slice_fusion.9
  140.4 6.0 %collective-permute-start.9 = (bf16[256,640]{0,1:T(8,128)(2,1)S(1)}, bf16[256,640]{0,1:T(8,128)(2,1)S(1)}, u32[]{:S(2)}, u32[]{:S(2)}) collective-permute-start(bf16[256,640]{0,1:T(8,128)(2,1)S(1)} %get-tuple-element.119), channel_id=1, source_target_pairs={{0,128},{8,136},{16,144},{24,152},{32,160},{40,168},{48,176},{56,1... | collective-permute-start | bytes 983048 | tf_op jit(solution)/shard_map/ppermute | solution.py:16
  149.4 5.9 %collective-permute-start.21 = (bf16[256,640]{0,1:T(8,128)(2,1)S(1)}, bf16[256,640]{0,1:T(8,128)(2,1)S(1)}, u32[]{:S(2)}, u32[]{:S(2)}) collective-permute-start(bf16[256,640]{0,1:T(8,128)(2,1)S(1)} %copy.85), channel_id=1, source_target_pairs={{0,128},{8,136},{16,144},{24,152},{32,160},{40,168},{48,176},{56,1... | collective-permute-start | bytes 983048 | tf_op jit(solution)/shard_map/ppermute | solution.py:16
  157.9 8.5 %collective-permute-start.11 = (bf16[256,640]{0,1:T(8,128)(2,1)S(1)}, bf16[256,640]{0,1:T(8,128)(2,1)S(1)}, u32[]{:S(2)}, u32[]{:S(2)}) collective-permute-start(bf16[256,640]{0,1:T(8,128)(2,1)S(1)} %get-tuple-element.119), channel_id=1, source_target_pairs={{0,256},{8,264},{16,272},{24,280},{32,288},{40,296},{48,304},{56,3... | collective-permute-start | bytes 983048 | tf_op jit(solution)/shard_map/ppermute | solution.py:16
  168.9 1.5 collective-permute-done.20
  170.4 32.8 %collective-permute-start.23 = (bf16[256,640]{0,1:T(8,128)(2,1)S(1)}, bf16[256,640]{0,1:T(8,128)(2,1)S(1)}, u32[]{:S(2)}, u32[]{:S(2)}) collective-permute-start(bf16[256,640]{0,1:T(8,128)(2,1)S(1)} %copy.85), channel_id=1, source_target_pairs={{0,256},{8,264},{16,272},{24,280},{32,288},{40,296},{48,304},{56,3... | collective-permute-start | bytes 983048 | tf_op jit(solution)/shard_map/ppermute | solution.py:16
  203.3 1.4 select_dynamic-update-slice_fusion.7
  204.7 1.4 select_dynamic-update-slice_fusion.1
  207.4 8.7 %collective-permute-done.23 = bf16[256,640]{0,1:T(8,128)(2,1)S(1)} collective-permute-done((bf16[256,640]{0,1:T(8,128)(2,1)S(1)}, bf16[256,640]{0,1:T(8,128)(2,1)S(1)}, u32[]{:S(2)}, u32[]{:S(2)}) %collective-permute-start.23) | collective-permute-done | bytes 327712 | tf_op jit(solution)/shard_map/ppermute | solution.py:16
  216.2 1.4 select_dynamic-update-slice_fusion
  217.6 58.0 %while.16 = (s32[]{:T(128)}, bf16[5,256,128]{1,2,0:T(8,128)(2,1)S(1)}, f32[5,256,128]{1,2,0:T(8,128)}, f32[5,1024,128]{1,2,0:T(8,128)}, f32[5,1024,128]{1,2,0:T(...) while((s32[]{:T(128)}, ...), condition=%wide.region_8.9_spmd, body=%wide.region_4.8_spmd.sunk | while | flops 406126080 | bytes 17450200 | solution.py:103
  217.6 1.5 fusion.79
  225.0 2.1 fusion.83
  229.2 1.5 fusion.79
  236.6 2.1 fusion.83
  240.8 1.5 fusion.79
  248.2 2.1 fusion.83
  252.3 1.5 fusion.79
  259.8 2.1 fusion.83
  263.9 1.5 fusion.79
  271.4 2.1 fusion.83
  275.6 1.9 bitcast_convert_fusion.1
  277.5 5.0 broadcast_select_fusion.2
  282.5 1.9 collective-permute-start.24
  285.5 3.1 collective-permute-start.25
  288.6 2.0 collective-permute-start.26
  291.9 2.4 collective-permute-start.28
  294.5 5.0 broadcast_select_fusion
  300.4 1.5 fusion.47
  301.9 5.5 collective-permute-start.36
  308.3 1.6 collective-permute-done.36
  311.3 2.1 collective-permute-start.37
  314.4 5.8 collective-permute-done.37
  320.2 4.0 collective-permute-start.30
  324.3 3.3 collective-permute-start.38
  328.6 2.3 collective-permute-done.38
  334.5 6.1 %collective-permute-done.39 = bf16[128,640]{0,1:T(8,128)(2,1)S(1)} collective-permute-done((bf16[128,640]{0,1:T(8,128)(2,1)S(1)}, bf16[128,640]{0,1:T(8,128)(2,1)S(1)}, u32[]{:S(2)}, u32[]{:S(2)}) %collective-permute-start.39) | collective-permute-done | bytes 163872 | tf_op jit(solution)/shard_map/ppermute | solution.py:16
  340.6 14.1 %collective-permute-start.32 = (bf16[128,640]{0,1:T(8,128)(2,1)S(1)}, bf16[128,640]{0,1:T(8,128)(2,1)S(1)}, u32[]{:S(2)}, u32[]{:S(2)}) collective-permute-start(bf16[128,640]{0,1:T(8,128)(2,1)S(1)} %bitcast.167), channel_id=1, source_target_pairs={{0,128},{8,136},{16,144},{24,152},{32,160},{40,168},{48,176},{56,1... | collective-permute-start | bytes 491528 | tf_op jit(solution)/shard_map/ppermute | solution.py:16
  354.8 7.0 %collective-permute-start.40 = (bf16[128,640]{0,1:T(8,128)(2,1)S(1)}, bf16[128,640]{0,1:T(8,128)(2,1)S(1)}, u32[]{:S(2)}, u32[]{:S(2)}) collective-permute-start(bf16[128,640]{0,1:T(8,128)(2,1)S(1)} %bitcast.176), channel_id=1, source_target_pairs={{0,32},{8,40},{16,48},{24,56},{32,64},{40,72},{48,80},{56,88},{64,... | collective-permute-start | bytes 491528 | tf_op jit(solution)/shard_map/ppermute | solution.py:16
  366.8 7.1 %collective-permute-done.41 = bf16[128,640]{0,1:T(8,128)(2,1)S(1)} collective-permute-done((bf16[128,640]{0,1:T(8,128)(2,1)S(1)}, bf16[128,640]{0,1:T(8,128)(2,1)S(1)}, u32[]{:S(2)}, u32[]{:S(2)}) %collective-permute-start.41) | collective-permute-done | bytes 163872 | tf_op jit(solution)/shard_map/ppermute | solution.py:16
  373.9 12.1 %collective-permute-start.34 = (bf16[128,640]{0,1:T(8,128)(2,1)S(1)}, bf16[128,640]{0,1:T(8,128)(2,1)S(1)}, u32[]{:S(2)}, u32[]{:S(2)}) collective-permute-start(bf16[128,640]{0,1:T(8,128)(2,1)S(1)} %bitcast.163), channel_id=1, source_target_pairs={{0,256},{8,264},{16,272},{24,280},{32,288},{40,296},{48,304},{56,3... | collective-permute-start | bytes 491528 | tf_op jit(solution)/shard_map/ppermute | solution.py:16
  386.2 6.0 %collective-permute-start.42 = (bf16[128,640]{0,1:T(8,128)(2,1)S(1)}, bf16[128,640]{0,1:T(8,128)(2,1)S(1)}, u32[]{:S(2)}, u32[]{:S(2)}) collective-permute-start(bf16[128,640]{0,1:T(8,128)(2,1)S(1)} %bitcast.174), channel_id=1, source_target_pairs={{0,64},{8,72},{16,80},{24,88},{32,96},{40,104},{48,112},{56,120},{... | collective-permute-start | bytes 491528 | tf_op jit(solution)/shard_map/ppermute | solution.py:16
  392.2 2.8 collective-permute-done.42
  397.8 5.5 collective-permute-done.43
  403.3 8.4 %collective-permute-start.44 = (bf16[128,640]{0,1:T(8,128)(2,1)S(1)}, bf16[128,640]{0,1:T(8,128)(2,1)S(1)}, u32[]{:S(2)}, u32[]{:S(2)}) collective-permute-start(bf16[128,640]{0,1:T(8,128)(2,1)S(1)} %bitcast.170), channel_id=1, source_target_pairs={{0,128},{8,136},{16,144},{24,152},{32,160},{40,168},{48,176},{56,1... | collective-permute-start | bytes 491528 | tf_op jit(solution)/shard_map/ppermute | solution.py:16
  413.9 11.1 %collective-permute-start.46 = (bf16[128,640]{0,1:T(8,128)(2,1)S(1)}, bf16[128,640]{0,1:T(8,128)(2,1)S(1)}, u32[]{:S(2)}, u32[]{:S(2)}) collective-permute-start(bf16[128,640]{0,1:T(8,128)(2,1)S(1)} %bitcast.166), channel_id=1, source_target_pairs={{0,256},{8,264},{16,272},{24,280},{32,288},{40,296},{48,304},{56,3... | collective-permute-start | bytes 491528 | tf_op jit(solution)/shard_map/ppermute | solution.py:16
  427.8 8.6 %collective-permute-done.47 = bf16[128,640]{0,1:T(8,128)(2,1)S(1)} collective-permute-done((bf16[128,640]{0,1:T(8,128)(2,1)S(1)}, bf16[128,640]{0,1:T(8,128)(2,1)S(1)}, u32[]{:S(2)}, u32[]{:S(2)}) %collective-permute-start.47) | collective-permute-done | bytes 163872 | tf_op jit(solution)/shard_map/ppermute | solution.py:16
  437.4 10.7 %all-reduce.1 = (f32[256]{0:T(256)S(1)}, f32[256]{0:T(256)S(1)}) all-reduce(f32[256]{0:T(256)S(1)} %get-tuple-element.93, f32[256]{0:T(256)S(1)} %get-tuple-element.91), channel_id=1, replica_groups=mesh['ctx'=64,'tp'=8] {'tp'}, use_global_device_ids=true, to_apply=%region_10.11 | all-reduce | flops 512 | bytes 4096 | tf_op jit(solution)/shard_map/psum | solution.py:139
  451.4 136.1 %all-reduce = (f32[640]{0:T(1024)}, f32[640]{0:T(1024)}) all-reduce(f32[640]{0:T(1024)S(1)} %get-tuple-element.92, f32[640]{0:T(1024)S(1)} %get-tuple-element.90), channel_id=1, replica_groups=mesh['ctx'=64,'tp'=8] {'ctx'}, use_global_device_ids=true, to_apply=%region_14.15 | all-reduce | flops 1280 | bytes 10240 | tf_op jit(solution)/shard_map/psum | solution.py:150
  (249 shorter events, 95.3 us)
Async XLA Ops:
  0.6 22.9 %copy-start.18 = (f32[640]{0:T(1024)S(1)}, f32[640]{0:T(1024)}, u32[]{:S(2)}) copy-start(f32[640]{0:T(1024)} %param.14) | copy-start | bytes 7684
  1.8 39.3 %copy-start.19 = (f32[640]{0:T(1024)S(1)}, f32[640]{0:T(1024)}, u32[]{:S(2)}) copy-start(f32[640]{0:T(1024)} %param.13) | copy-start | bytes 7684
  1.9 40.1 %copy-start.21 = (s32[1,6]{1,0:T(1,128)S(1)}, s32[1,6]{1,0:T(1,128)}, u32[]{:S(2)}) copy-start(s32[1,6]{1,0:T(1,128)} %param.16) | copy-start | bytes 76
  1.9 40.1 %copy-start.20 = (s32[1,6]{1,0:T(1,128)S(1)}, s32[1,6]{1,0:T(1,128)}, u32[]{:S(2)}) copy-start(s32[1,6]{1,0:T(1,128)} %param.17) | copy-start | bytes 76
  3.1 92.4 %copy-start.3 = (bf16[256,640]{1,0:T(8,128)(2,1)S(1)}, bf16[256,640]{1,0:T(8,128)(2,1)}, u32[]{:S(2)}) copy-start(bf16[256,640]{1,0:T(8,128)(2,1)} %param.12) | copy-start | bytes 983044
  23.5 72.2 %copy-start.4 = (bf16[256,640]{1,0:T(8,128)(2,1)S(1)}, bf16[256,640]{1,0:T(8,128)(2,1)}, u32[]{:S(2)}) copy-start(bf16[256,640]{1,0:T(8,128)(2,1)} %param.15) | copy-start | bytes 983044
  24.4 71.5 %collective-permute-start = (bf16[256,640]{0,1:T(8,128)(2,1)S(1)}, bf16[256,640]{0,1:T(8,128)(2,1)}, u32[]{:S(2)}, u32[]{:S(2)}) collective-permute-start(bf16[256,640]{0,1:T(8,128)(2,1)S(1)} %get-tuple-element.119), channel_id=1, source_target_pairs={{8,0},{16,8},{24,16},{32,24},{40,32},{48,40},{56,48},{64,56},{72,6... | collective-permute-start | bytes 983048 | tf_op jit(solution)/shard_map/ppermute | solution.py:16
  30.8 67.3 %collective-permute-start.1 = (bf16[256,640]{0,1:T(8,128)(2,1)S(1)}, bf16[256,640]{0,1:T(8,128)(2,1)}, u32[]{:S(2)}, u32[]{:S(2)}) collective-permute-start(bf16[256,640]{0,1:T(8,128)(2,1)S(1)} %get-tuple-element.119), channel_id=1, source_target_pairs={{0,8},{8,16},{16,24},{24,32},{32,40},{40,48},{48,56},{56,64},{64,7... | collective-permute-start | bytes 983048 | tf_op jit(solution)/shard_map/ppermute | solution.py:16
  33.8 68.6 %collective-permute-start.2 = (bf16[256,640]{0,1:T(8,128)(2,1)S(1)}, bf16[256,640]{0,1:T(8,128)(2,1)S(1)}, u32[]{:S(2)}, u32[]{:S(2)}) collective-permute-start(bf16[256,640]{0,1:T(8,128)(2,1)S(1)} %get-tuple-element.119), channel_id=1, source_target_pairs={{16,0},{24,8},{32,16},{40,24},{48,32},{56,40},{64,48},{72,56},{80,... | collective-permute-start | bytes 983048 | tf_op jit(solution)/shard_map/ppermute | solution.py:16
  35.1 70.5 %collective-permute-start.3 = (bf16[256,640]{0,1:T(8,128)(2,1)S(1)}, bf16[256,640]{0,1:T(8,128)(2,1)}, u32[]{:S(2)}, u32[]{:S(2)}) collective-permute-start(bf16[256,640]{0,1:T(8,128)(2,1)S(1)} %get-tuple-element.119), channel_id=1, source_target_pairs={{0,16},{8,24},{16,32},{24,40},{32,48},{40,56},{48,64},{56,72},{64,... | collective-permute-start | bytes 983048 | tf_op jit(solution)/shard_map/ppermute | solution.py:16
  39.8 67.7 %collective-permute-start.4 = (bf16[256,640]{0,1:T(8,128)(2,1)S(1)}, bf16[256,640]{0,1:T(8,128)(2,1)S(1)}, u32[]{:S(2)}, u32[]{:S(2)}) collective-permute-start(bf16[256,640]{0,1:T(8,128)(2,1)S(1)} %get-tuple-element.119), channel_id=1, source_target_pairs={{32,0},{40,8},{48,16},{56,24},{64,32},{72,40},{80,48},{88,56},{96,... | collective-permute-start | bytes 983048 | tf_op jit(solution)/shard_map/ppermute | solution.py:16
  96.0 19.3 %collective-permute-start.12 = (bf16[256,640]{0,1:T(8,128)(2,1)S(1)}, bf16[256,640]{0,1:T(8,128)(2,1)S(1)}, u32[]{:S(2)}, u32[]{:S(2)}) collective-permute-start(bf16[256,640]{0,1:T(8,128)(2,1)S(1)} %copy.85), channel_id=1, source_target_pairs={{8,0},{16,8},{24,16},{32,24},{40,32},{48,40},{56,48},{64,56},{72,6... | collective-permute-start | bytes 983048 | tf_op jit(solution)/shard_map/ppermute | solution.py:16
  98.0 18.5 %collective-permute-start.13 = (bf16[256,640]{0,1:T(8,128)(2,1)S(1)}, bf16[256,640]{0,1:T(8,128)(2,1)S(1)}, u32[]{:S(2)}, u32[]{:S(2)}) collective-permute-start(bf16[256,640]{0,1:T(8,128)(2,1)S(1)} %copy.85), channel_id=1, source_target_pairs={{0,8},{8,16},{16,24},{24,32},{32,40},{40,48},{48,56},{56,64},{64,7... | collective-permute-start | bytes 983048 | tf_op jit(solution)/shard_map/ppermute | solution.py:16
  102.3 19.5 %collective-permute-start.5 = (bf16[256,640]{0,1:T(8,128)(2,1)S(1)}, bf16[256,640]{0,1:T(8,128)(2,1)S(1)}, u32[]{:S(2)}, u32[]{:S(2)}) collective-permute-start(bf16[256,640]{0,1:T(8,128)(2,1)S(1)} %get-tuple-element.119), channel_id=1, source_target_pairs={{0,32},{8,40},{16,48},{24,56},{32,64},{40,72},{48,80},{56,88},{64,... | collective-permute-start | bytes 983048 | tf_op jit(solution)/shard_map/ppermute | solution.py:16
  105.6 17.6 %collective-permute-start.14 = (bf16[256,640]{0,1:T(8,128)(2,1)S(1)}, bf16[256,640]{0,1:T(8,128)(2,1)S(1)}, u32[]{:S(2)}, u32[]{:S(2)}) collective-permute-start(bf16[256,640]{0,1:T(8,128)(2,1)S(1)} %copy.85), channel_id=1, source_target_pairs={{16,0},{24,8},{32,16},{40,24},{48,32},{56,40},{64,48},{72,56},{80,... | collective-permute-start | bytes 983048 | tf_op jit(solution)/shard_map/ppermute | solution.py:16
  107.6 23.5 %collective-permute-start.15 = (bf16[256,640]{0,1:T(8,128)(2,1)S(1)}, bf16[256,640]{0,1:T(8,128)(2,1)S(1)}, u32[]{:S(2)}, u32[]{:S(2)}) collective-permute-start(bf16[256,640]{0,1:T(8,128)(2,1)S(1)} %copy.85), channel_id=1, source_target_pairs={{0,16},{8,24},{16,32},{24,40},{32,48},{40,56},{48,64},{56,72},{64,... | collective-permute-start | bytes 983048 | tf_op jit(solution)/shard_map/ppermute | solution.py:16
  115.3 18.5 %collective-permute-start.6 = (bf16[256,640]{0,1:T(8,128)(2,1)S(1)}, bf16[256,640]{0,1:T(8,128)(2,1)S(1)}, u32[]{:S(2)}, u32[]{:S(2)}) collective-permute-start(bf16[256,640]{0,1:T(8,128)(2,1)S(1)} %get-tuple-element.119), channel_id=1, source_target_pairs={{64,0},{72,8},{80,16},{88,24},{96,32},{104,40},{112,48},{120,56},{... | collective-permute-start | bytes 983048 | tf_op jit(solution)/shard_map/ppermute | solution.py:16
  116.6 18.5 %collective-permute-start.7 = (bf16[256,640]{0,1:T(8,128)(2,1)S(1)}, bf16[256,640]{0,1:T(8,128)(2,1)S(1)}, u32[]{:S(2)}, u32[]{:S(2)}) collective-permute-start(bf16[256,640]{0,1:T(8,128)(2,1)S(1)} %get-tuple-element.119), channel_id=1, source_target_pairs={{0,64},{8,72},{16,80},{24,88},{32,96},{40,104},{48,112},{56,120},{... | collective-permute-start | bytes 983048 | tf_op jit(solution)/shard_map/ppermute | solution.py:16
  121.9 18.6 %collective-permute-start.16 = (bf16[256,640]{0,1:T(8,128)(2,1)S(1)}, bf16[256,640]{0,1:T(8,128)(2,1)S(1)}, u32[]{:S(2)}, u32[]{:S(2)}) collective-permute-start(bf16[256,640]{0,1:T(8,128)(2,1)S(1)} %copy.85), channel_id=1, source_target_pairs={{32,0},{40,8},{48,16},{56,24},{64,32},{72,40},{80,48},{88,56},{96,... | collective-permute-start | bytes 983048 | tf_op jit(solution)/shard_map/ppermute | solution.py:16
  123.2 23.3 %collective-permute-start.17 = (bf16[256,640]{0,1:T(8,128)(2,1)S(1)}, bf16[256,640]{0,1:T(8,128)(2,1)S(1)}, u32[]{:S(2)}, u32[]{:S(2)}) collective-permute-start(bf16[256,640]{0,1:T(8,128)(2,1)S(1)} %copy.85), channel_id=1, source_target_pairs={{0,32},{8,40},{16,48},{24,56},{32,64},{40,72},{48,80},{56,88},{64,... | collective-permute-start | bytes 983048 | tf_op jit(solution)/shard_map/ppermute | solution.py:16
  131.0 18.3 %collective-permute-start.8 = (bf16[256,640]{0,1:T(8,128)(2,1)S(1)}, bf16[256,640]{0,1:T(8,128)(2,1)S(1)}, u32[]{:S(2)}, u32[]{:S(2)}) collective-permute-start(bf16[256,640]{0,1:T(8,128)(2,1)S(1)} %get-tuple-element.119), channel_id=1, source_target_pairs={{128,0},{136,8},{144,16},{152,24},{160,32},{168,40},{176,48},{184,... | collective-permute-start | bytes 983048 | tf_op jit(solution)/shard_map/ppermute | solution.py:16
  133.7 22.8 %collective-permute-start.18 = (bf16[256,640]{0,1:T(8,128)(2,1)S(1)}, bf16[256,640]{0,1:T(8,128)(2,1)S(1)}, u32[]{:S(2)}, u32[]{:S(2)}) collective-permute-start(bf16[256,640]{0,1:T(8,128)(2,1)S(1)} %copy.85), channel_id=1, source_target_pairs={{64,0},{72,8},{80,16},{88,24},{96,32},{104,40},{112,48},{120,56},{... | collective-permute-start | bytes 983048 | tf_op jit(solution)/shard_map/ppermute | solution.py:16
  135.0 22.8 %collective-permute-start.19 = (bf16[256,640]{0,1:T(8,128)(2,1)S(1)}, bf16[256,640]{0,1:T(8,128)(2,1)S(1)}, u32[]{:S(2)}, u32[]{:S(2)}) collective-permute-start(bf16[256,640]{0,1:T(8,128)(2,1)S(1)} %copy.85), channel_id=1, source_target_pairs={{0,64},{8,72},{16,80},{24,88},{32,96},{40,104},{48,112},{56,120},{... | collective-permute-start | bytes 983048 | tf_op jit(solution)/shard_map/ppermute | solution.py:16
  140.4 27.2 %collective-permute-start.9 = (bf16[256,640]{0,1:T(8,128)(2,1)S(1)}, bf16[256,640]{0,1:T(8,128)(2,1)S(1)}, u32[]{:S(2)}, u32[]{:S(2)}) collective-permute-start(bf16[256,640]{0,1:T(8,128)(2,1)S(1)} %get-tuple-element.119), channel_id=1, source_target_pairs={{0,128},{8,136},{16,144},{24,152},{32,160},{40,168},{48,176},{56,1... | collective-permute-start | bytes 983048 | tf_op jit(solution)/shard_map/ppermute | solution.py:16
  146.5 23.9 %collective-permute-start.20 = (bf16[256,640]{0,1:T(8,128)(2,1)S(1)}, bf16[256,640]{0,1:T(8,128)(2,1)S(1)}, u32[]{:S(2)}, u32[]{:S(2)}) collective-permute-start(bf16[256,640]{0,1:T(8,128)(2,1)S(1)} %copy.85), channel_id=1, source_target_pairs={{128,0},{136,8},{144,16},{152,24},{160,32},{168,40},{176,48},{184,... | collective-permute-start | bytes 983048 | tf_op jit(solution)/shard_map/ppermute | solution.py:16
  149.4 55.3 %collective-permute-start.21 = (bf16[256,640]{0,1:T(8,128)(2,1)S(1)}, bf16[256,640]{0,1:T(8,128)(2,1)S(1)}, u32[]{:S(2)}, u32[]{:S(2)}) collective-permute-start(bf16[256,640]{0,1:T(8,128)(2,1)S(1)} %copy.85), channel_id=1, source_target_pairs={{0,128},{8,136},{16,144},{24,152},{32,160},{40,168},{48,176},{56,1... | collective-permute-start | bytes 983048 | tf_op jit(solution)/shard_map/ppermute | solution.py:16
  156.6 49.5 %collective-permute-start.10 = (bf16[256,640]{0,1:T(8,128)(2,1)S(1)}, bf16[256,640]{0,1:T(8,128)(2,1)S(1)}, u32[]{:S(2)}, u32[]{:S(2)}) collective-permute-start(bf16[256,640]{0,1:T(8,128)(2,1)S(1)} %get-tuple-element.119), channel_id=1, source_target_pairs={{256,0},{264,8},{272,16},{280,24},{288,32},{296,40},{304,48},{312,... | collective-permute-start | bytes 983048 | tf_op jit(solution)/shard_map/ppermute | solution.py:16
  157.9 48.2 %collective-permute-start.11 = (bf16[256,640]{0,1:T(8,128)(2,1)S(1)}, bf16[256,640]{0,1:T(8,128)(2,1)S(1)}, u32[]{:S(2)}, u32[]{:S(2)}) collective-permute-start(bf16[256,640]{0,1:T(8,128)(2,1)S(1)} %get-tuple-element.119), channel_id=1, source_target_pairs={{0,256},{8,264},{16,272},{24,280},{32,288},{40,296},{48,304},{56,3... | collective-permute-start | bytes 983048 | tf_op jit(solution)/shard_map/ppermute | solution.py:16
  167.7 39.8 %collective-permute-start.22 = (bf16[256,640]{0,1:T(8,128)(2,1)S(1)}, bf16[256,640]{0,1:T(8,128)(2,1)S(1)}, u32[]{:S(2)}, u32[]{:S(2)}) collective-permute-start(bf16[256,640]{0,1:T(8,128)(2,1)S(1)} %copy.85), channel_id=1, source_target_pairs={{256,0},{264,8},{272,16},{280,24},{288,32},{296,40},{304,48},{312,... | collective-permute-start | bytes 983048 | tf_op jit(solution)/shard_map/ppermute | solution.py:16
  170.4 45.7 %collective-permute-start.23 = (bf16[256,640]{0,1:T(8,128)(2,1)S(1)}, bf16[256,640]{0,1:T(8,128)(2,1)S(1)}, u32[]{:S(2)}, u32[]{:S(2)}) collective-permute-start(bf16[256,640]{0,1:T(8,128)(2,1)S(1)} %copy.85), channel_id=1, source_target_pairs={{0,256},{8,264},{16,272},{24,280},{32,288},{40,296},{48,304},{56,3... | collective-permute-start | bytes 983048 | tf_op jit(solution)/shard_map/ppermute | solution.py:16
  277.5 16.7 %copy-start.2 = (f32[5,1024,128]{1,2,0:T(8,128)S(1)}, f32[5,1024,128]{1,2,0:T(8,128)}, u32[]{:S(2)}) copy-start(f32[5,1024,128]{1,2,0:T(8,128)} %get-tuple-element.59) | copy-start | bytes 7864324
  282.5 19.4 %collective-permute-start.24 = (bf16[128,640]{0,1:T(8,128)(2,1)}, bf16[128,640]{0,1:T(8,128)(2,1)}, u32[]{:S(2)}, u32[]{:S(2)}) collective-permute-start(bf16[128,640]{0,1:T(8,128)(2,1)} %bitcast.37), channel_id=1, source_target_pairs={{0,8},{8,16},{16,24},{24,32},{32,40},{40,48},{48,56},{56,64},{64,7... | collective-permute-start | bytes 491528 | tf_op jit(solution)/shard_map/ppermute | solution.py:16
  285.5 25.8 %collective-permute-start.25 = (bf16[128,640]{0,1:T(8,128)(2,1)}, bf16[128,640]{0,1:T(8,128)(2,1)}, u32[]{:S(2)}, u32[]{:S(2)}) collective-permute-start(bf16[128,640]{0,1:T(8,128)(2,1)} %bitcast.39), channel_id=1, source_target_pairs={{8,0},{16,8},{24,16},{32,24},{40,32},{48,40},{56,48},{64,56},{72,6... | collective-permute-start | bytes 491528 | tf_op jit(solution)/shard_map/ppermute | solution.py:16
  288.6 35.6 %collective-permute-start.26 = (bf16[128,640]{0,1:T(8,128)(2,1)}, bf16[128,640]{0,1:T(8,128)(2,1)}, u32[]{:S(2)}, u32[]{:S(2)}) collective-permute-start(bf16[128,640]{0,1:T(8,128)(2,1)} %bitcast.41), channel_id=1, source_target_pairs={{0,16},{8,24},{16,32},{24,40},{32,48},{40,56},{48,64},{56,72},{64,... | collective-permute-start | bytes 491528 | tf_op jit(solution)/shard_map/ppermute | solution.py:16
  290.6 41.7 %collective-permute-start.27 = (bf16[128,640]{0,1:T(8,128)(2,1)}, bf16[128,640]{0,1:T(8,128)(2,1)}, u32[]{:S(2)}, u32[]{:S(2)}) collective-permute-start(bf16[128,640]{0,1:T(8,128)(2,1)} %bitcast.43), channel_id=1, source_target_pairs={{16,0},{24,8},{32,16},{40,24},{48,32},{56,40},{64,48},{72,56},{80,... | collective-permute-start | bytes 491528 | tf_op jit(solution)/shard_map/ppermute | solution.py:16
  291.9 62.9 %collective-permute-start.28 = (bf16[128,640]{0,1:T(8,128)(2,1)}, bf16[128,640]{0,1:T(8,128)(2,1)}, u32[]{:S(2)}, u32[]{:S(2)}) collective-permute-start(bf16[128,640]{0,1:T(8,128)(2,1)} %bitcast.45), channel_id=1, source_target_pairs={{0,32},{8,40},{16,48},{24,56},{32,64},{40,72},{48,80},{56,88},{64,... | collective-permute-start | bytes 491528 | tf_op jit(solution)/shard_map/ppermute | solution.py:16
  301.9 18.3 %copy-start.9 = (bf16[128,5,128]{0,2,1:T(8,128)(2,1)S(1)}, bf16[128,5,128]{0,2,1:T(8,128)(2,1)}, u32[]{:S(2)}) copy-start(bf16[128,5,128]{0,2,1:T(8,128)(2,1)} %get-tuple-element.143) | copy-start | bytes 491524
  301.9 8.0 %collective-permute-start.36 = (bf16[128,640]{0,1:T(8,128)(2,1)}, bf16[128,640]{0,1:T(8,128)(2,1)S(1)}, u32[]{:S(2)}, u32[]{:S(2)}) collective-permute-start(bf16[128,640]{0,1:T(8,128)(2,1)} %bitcast.180), channel_id=1, source_target_pairs={{0,8},{8,16},{16,24},{24,32},{32,40},{40,48},{48,56},{56,64},{64,7... | collective-permute-start | bytes 491528 | tf_op jit(solution)/shard_map/ppermute | solution.py:16
  308.3 15.9 %copy-start.16 = (bf16[128,5,128]{0,2,1:T(8,128)(2,1)S(1)}, bf16[128,5,128]{0,2,1:T(8,128)(2,1)}, u32[]{:S(2)}) copy-start(bf16[128,5,128]{0,2,1:T(8,128)(2,1)} %get-tuple-element.133) | copy-start | bytes 491524
  309.9 55.5 %collective-permute-start.29 = (bf16[128,640]{0,1:T(8,128)(2,1)S(1)}, bf16[128,640]{0,1:T(8,128)(2,1)S(1)}, u32[]{:S(2)}, u32[]{:S(2)}) collective-permute-start(bf16[128,640]{0,1:T(8,128)(2,1)S(1)} %bitcast.173), channel_id=1, source_target_pairs={{32,0},{40,8},{48,16},{56,24},{64,32},{72,40},{80,48},{88,56},{96,... | collective-permute-start | bytes 491528 | tf_op jit(solution)/shard_map/ppermute | solution.py:16
  311.3 19.6 %copy-start.7 = (bf16[128,5,128]{0,2,1:T(8,128)(2,1)S(1)}, bf16[128,5,128]{0,2,1:T(8,128)(2,1)}, u32[]{:S(2)}) copy-start(bf16[128,5,128]{0,2,1:T(8,128)(2,1)} %get-tuple-element.140) | copy-start | bytes 491524
  311.3 8.9 %collective-permute-start.37 = (bf16[128,640]{0,1:T(8,128)(2,1)S(1)}, bf16[128,640]{0,1:T(8,128)(2,1)S(1)}, u32[]{:S(2)}, u32[]{:S(2)}) collective-permute-start(bf16[128,640]{0,1:T(8,128)(2,1)S(1)} %bitcast.179), channel_id=1, source_target_pairs={{8,0},{16,8},{24,16},{32,24},{40,32},{48,40},{56,48},{64,56},{72,6... | collective-permute-start | bytes 491528 | tf_op jit(solution)/shard_map/ppermute | solution.py:16
  314.3 17.9 %copy-start.15 = (bf16[128,5,128]{0,2,1:T(8,128)(2,1)S(1)}, bf16[128,5,128]{0,2,1:T(8,128)(2,1)}, u32[]{:S(2)}) copy-start(bf16[128,5,128]{0,2,1:T(8,128)(2,1)} %get-tuple-element.126) | copy-start | bytes 491524
  320.2 66.0 %collective-permute-start.30 = (bf16[128,640]{0,1:T(8,128)(2,1)S(1)}, bf16[128,640]{0,1:T(8,128)(2,1)S(1)}, u32[]{:S(2)}, u32[]{:S(2)}) collective-permute-start(bf16[128,640]{0,1:T(8,128)(2,1)S(1)} %bitcast.171), channel_id=1, source_target_pairs={{0,64},{8,72},{16,80},{24,88},{32,96},{40,104},{48,112},{56,120},{... | collective-permute-start | bytes 491528 | tf_op jit(solution)/shard_map/ppermute | solution.py:16
  324.3 6.6 %collective-permute-start.38 = (bf16[128,640]{0,1:T(8,128)(2,1)S(1)}, bf16[128,640]{0,1:T(8,128)(2,1)S(1)}, u32[]{:S(2)}, u32[]{:S(2)}) collective-permute-start(bf16[128,640]{0,1:T(8,128)(2,1)S(1)} %bitcast.178), channel_id=1, source_target_pairs={{0,16},{8,24},{16,32},{24,40},{32,48},{40,56},{48,64},{56,72},{64,... | collective-permute-start | bytes 491528 | tf_op jit(solution)/shard_map/ppermute | solution.py:16
  328.6 26.2 %copy-start.14 = (bf16[128,5,128]{0,2,1:T(8,128)(2,1)S(1)}, bf16[128,5,128]{0,2,1:T(8,128)(2,1)}, u32[]{:S(2)}) copy-start(bf16[128,5,128]{0,2,1:T(8,128)(2,1)} %get-tuple-element.132) | copy-start | bytes 491524
  330.9 65.5 %collective-permute-start.31 = (bf16[128,640]{0,1:T(8,128)(2,1)S(1)}, bf16[128,640]{0,1:T(8,128)(2,1)S(1)}, u32[]{:S(2)}, u32[]{:S(2)}) collective-permute-start(bf16[128,640]{0,1:T(8,128)(2,1)S(1)} %bitcast.169), channel_id=1, source_target_pairs={{64,0},{72,8},{80,16},{88,24},{96,32},{104,40},{112,48},{120,56},{... | collective-permute-start | bytes 491528 | tf_op jit(solution)/shard_map/ppermute | solution.py:16
  332.2 8.4 %collective-permute-start.39 = (bf16[128,640]{0,1:T(8,128)(2,1)S(1)}, bf16[128,640]{0,1:T(8,128)(2,1)S(1)}, u32[]{:S(2)}, u32[]{:S(2)}) collective-permute-start(bf16[128,640]{0,1:T(8,128)(2,1)S(1)} %bitcast.177), channel_id=1, source_target_pairs={{16,0},{24,8},{32,16},{40,24},{48,32},{56,40},{64,48},{72,56},{80,... | collective-permute-start | bytes 491528 | tf_op jit(solution)/shard_map/ppermute | solution.py:16
  334.5 30.9 %copy-start.13 = (bf16[128,5,128]{0,2,1:T(8,128)(2,1)S(1)}, bf16[128,5,128]{0,2,1:T(8,128)(2,1)}, u32[]{:S(2)}) copy-start(bf16[128,5,128]{0,2,1:T(8,128)(2,1)} %get-tuple-element.127) | copy-start | bytes 491524
  340.6 71.1 %collective-permute-start.32 = (bf16[128,640]{0,1:T(8,128)(2,1)S(1)}, bf16[128,640]{0,1:T(8,128)(2,1)S(1)}, u32[]{:S(2)}, u32[]{:S(2)}) collective-permute-start(bf16[128,640]{0,1:T(8,128)(2,1)S(1)} %bitcast.167), channel_id=1, source_target_pairs={{0,128},{8,136},{16,144},{24,152},{32,160},{40,168},{48,176},{56,1... | collective-permute-start | bytes 491528 | tf_op jit(solution)/shard_map/ppermute | solution.py:16
  354.8 9.2 %collective-permute-start.40 = (bf16[128,640]{0,1:T(8,128)(2,1)S(1)}, bf16[128,640]{0,1:T(8,128)(2,1)S(1)}, u32[]{:S(2)}, u32[]{:S(2)}) collective-permute-start(bf16[128,640]{0,1:T(8,128)(2,1)S(1)} %bitcast.176), channel_id=1, source_target_pairs={{0,32},{8,40},{16,48},{24,56},{32,64},{40,72},{48,80},{56,88},{64,... | collective-permute-start | bytes 491528 | tf_op jit(solution)/shard_map/ppermute | solution.py:16
  362.8 23.4 %copy-start.12 = (bf16[128,5,128]{0,2,1:T(8,128)(2,1)S(1)}, bf16[128,5,128]{0,2,1:T(8,128)(2,1)}, u32[]{:S(2)}) copy-start(bf16[128,5,128]{0,2,1:T(8,128)(2,1)} %get-tuple-element.131) | copy-start | bytes 491524
  364.0 61.0 %collective-permute-start.33 = (bf16[128,640]{0,1:T(8,128)(2,1)S(1)}, bf16[128,640]{0,1:T(8,128)(2,1)S(1)}, u32[]{:S(2)}, u32[]{:S(2)}) collective-permute-start(bf16[128,640]{0,1:T(8,128)(2,1)S(1)} %bitcast.165), channel_id=1, source_target_pairs={{128,0},{136,8},{144,16},{152,24},{160,32},{168,40},{176,48},{184,... | collective-permute-start | bytes 491528 | tf_op jit(solution)/shard_map/ppermute | solution.py:16
  365.4 8.5 %collective-permute-start.41 = (bf16[128,640]{0,1:T(8,128)(2,1)S(1)}, bf16[128,640]{0,1:T(8,128)(2,1)S(1)}, u32[]{:S(2)}, u32[]{:S(2)}) collective-permute-start(bf16[128,640]{0,1:T(8,128)(2,1)S(1)} %bitcast.175), channel_id=1, source_target_pairs={{32,0},{40,8},{48,16},{56,24},{64,32},{72,40},{80,48},{88,56},{96,... | collective-permute-start | bytes 491528 | tf_op jit(solution)/shard_map/ppermute | solution.py:16
  366.8 29.6 %copy-start.10 = (bf16[128,5,128]{0,2,1:T(8,128)(2,1)S(1)}, bf16[128,5,128]{0,2,1:T(8,128)(2,1)}, u32[]{:S(2)}) copy-start(bf16[128,5,128]{0,2,1:T(8,128)(2,1)} %get-tuple-element.128) | copy-start | bytes 491524
  373.9 52.6 %collective-permute-start.34 = (bf16[128,640]{0,1:T(8,128)(2,1)S(1)}, bf16[128,640]{0,1:T(8,128)(2,1)S(1)}, u32[]{:S(2)}, u32[]{:S(2)}) collective-permute-start(bf16[128,640]{0,1:T(8,128)(2,1)S(1)} %bitcast.163), channel_id=1, source_target_pairs={{0,256},{8,264},{16,272},{24,280},{32,288},{40,296},{48,304},{56,3... | collective-permute-start | bytes 491528 | tf_op jit(solution)/shard_map/ppermute | solution.py:16
  386.1 17.1 %copy-start.8 = (bf16[128,5,128]{0,2,1:T(8,128)(2,1)S(1)}, bf16[128,5,128]{0,2,1:T(8,128)(2,1)}, u32[]{:S(2)}) copy-start(bf16[128,5,128]{0,2,1:T(8,128)(2,1)} %get-tuple-element.130) | copy-start | bytes 491524
  386.2 8.9 %collective-permute-start.42 = (bf16[128,640]{0,1:T(8,128)(2,1)S(1)}, bf16[128,640]{0,1:T(8,128)(2,1)S(1)}, u32[]{:S(2)}, u32[]{:S(2)}) collective-permute-start(bf16[128,640]{0,1:T(8,128)(2,1)S(1)} %bitcast.174), channel_id=1, source_target_pairs={{0,64},{8,72},{16,80},{24,88},{32,96},{40,104},{48,112},{56,120},{... | collective-permute-start | bytes 491528 | tf_op jit(solution)/shard_map/ppermute | solution.py:16
  395.0 32.3 %collective-permute-start.35 = (bf16[128,640]{0,1:T(8,128)(2,1)S(1)}, bf16[128,640]{0,1:T(8,128)(2,1)S(1)}, u32[]{:S(2)}, u32[]{:S(2)}) collective-permute-start(bf16[128,640]{0,1:T(8,128)(2,1)S(1)} %bitcast.162), channel_id=1, source_target_pairs={{256,0},{264,8},{272,16},{280,24},{288,32},{296,40},{304,48},{312,... | collective-permute-start | bytes 491528 | tf_op jit(solution)/shard_map/ppermute | solution.py:16
  396.4 6.9 %collective-permute-start.43 = (bf16[128,640]{0,1:T(8,128)(2,1)S(1)}, bf16[128,640]{0,1:T(8,128)(2,1)S(1)}, u32[]{:S(2)}, u32[]{:S(2)}) collective-permute-start(bf16[128,640]{0,1:T(8,128)(2,1)S(1)} %bitcast.172), channel_id=1, source_target_pairs={{64,0},{72,8},{80,16},{88,24},{96,32},{104,40},{112,48},{120,56},{... | collective-permute-start | bytes 491528 | tf_op jit(solution)/shard_map/ppermute | solution.py:16
  403.3 10.6 %collective-permute-start.44 = (bf16[128,640]{0,1:T(8,128)(2,1)S(1)}, bf16[128,640]{0,1:T(8,128)(2,1)S(1)}, u32[]{:S(2)}, u32[]{:S(2)}) collective-permute-start(bf16[128,640]{0,1:T(8,128)(2,1)S(1)} %bitcast.170), channel_id=1, source_target_pairs={{0,128},{8,136},{16,144},{24,152},{32,160},{40,168},{48,176},{56,1... | collective-permute-start | bytes 491528 | tf_op jit(solution)/shard_map/ppermute | solution.py:16
  411.7 14.7 %collective-permute-start.45 = (bf16[128,640]{0,1:T(8,128)(2,1)S(1)}, bf16[128,640]{0,1:T(8,128)(2,1)S(1)}, u32[]{:S(2)}, u32[]{:S(2)}) collective-permute-start(bf16[128,640]{0,1:T(8,128)(2,1)S(1)} %bitcast.168), channel_id=1, source_target_pairs={{128,0},{136,8},{144,16},{152,24},{160,32},{168,40},{176,48},{184,... | collective-permute-start | bytes 491528 | tf_op jit(solution)/shard_map/ppermute | solution.py:16
  413.9 13.4 %collective-permute-start.46 = (bf16[128,640]{0,1:T(8,128)(2,1)S(1)}, bf16[128,640]{0,1:T(8,128)(2,1)S(1)}, u32[]{:S(2)}, u32[]{:S(2)}) collective-permute-start(bf16[128,640]{0,1:T(8,128)(2,1)S(1)} %bitcast.166), channel_id=1, source_target_pairs={{0,256},{8,264},{16,272},{24,280},{32,288},{40,296},{48,304},{56,3... | collective-permute-start | bytes 491528 | tf_op jit(solution)/shard_map/ppermute | solution.py:16
  425.1 11.3 %collective-permute-start.47 = (bf16[128,640]{0,1:T(8,128)(2,1)S(1)}, bf16[128,640]{0,1:T(8,128)(2,1)S(1)}, u32[]{:S(2)}, u32[]{:S(2)}) collective-permute-start(bf16[128,640]{0,1:T(8,128)(2,1)S(1)} %bitcast.164), channel_id=1, source_target_pairs={{256,0},{264,8},{272,16},{280,24},{288,32},{296,40},{304,48},{312,... | collective-permute-start | bytes 491528 | tf_op jit(solution)/shard_map/ppermute | solution.py:16
  (22 other events, 81.6 us)
where the time goes:
time: 591 us; the launch traced here: 588 us
  blocking collectives  208 us (35%)
  starting transfers between devices  204 us (35%)
  waiting for transfers between devices  53 us (9%)
  other arithmetic  43.5 us (7%)
  matrix products  43.4 us (7%)
  local copies, waits for them, and re-layouts  22.8 us (4%)
  between operations  13.2 us (2%)
    ppermute x48, starting transfers between devices, from_behind_2(): lax.ppermute(value, axis, [(source, source + steps) for source in range(l...  204 us
    psum x1, blocking collectives, per_device(): q_gain_grad, k_gain_grad = lax.psum((q_gain_grad, k_gain_grad), 'ctx')  136 us
    ppermute x48, waiting for transfers between devices, from_behind_2(): lax.ppermute(value, axis, [(source, source + steps) for source in range(l...  53 us
    all_gather x1, blocking collectives, per_device(): all_blocks = lax.all_gather(far_blocks, 'ctx', axis=0, tiled=True)  40.5 us
    psum x1, blocking collectives, per_device(): lax.psum((jnp.sum(q_float * q_float, axis=1), jnp.sum(k_float * k_float,...  20.3 us
    unnamed x11, other arithmetic  16.4 us
  transfers between devices with their start and end apart: 48, of which 14 were waited for; matrix products, arithmetic and copies ran while one was open for 6% of the time, Pallas kernels for 0%

commit v1 on v0

v1 whole, which is shorter than its diff:
```python
import functools

import jax
import jax.numpy as jnp
from jax import lax
from jax.experimental import pallas as pl
from jax.experimental.pallas import tpu as pltpu
from jax.sharding import Mesh
from jax.sharding import PartitionSpec as P

HD = 128
BLK = 128
EPS = 1e-06
SCALE = HD**-0.5
LOG2E = 1.4426950408889634
CTX = ("cy", "cx")
WAYS = tuple((band, other) for band in range(6) for other in range(2 if band < 5 else 1))
MIB = 1 << 20


ORDER = ((4, 0), (4, 1), (5, 0), (2, 0), (2, 1), (3, 0), (3, 1), (1, 0), (1, 1), (0, 0), (0, 1))
WINDOW = 5


def pairs_of(way, count=64):
    band, other = way
    stride = 1 << band
    lower = [f for f in range(count - stride) if (f >> band) & 1 == other]
    return [pair for f in lower for pair in ((f, f + stride), (f + stride, f))]


def move(value, way):
    return lax.ppermute(value, CTX, pairs_of(way))


def dot(a, b, dims):
    return lax.dot_general(a, b, (dims, ((), ())), preferred_element_type=jnp.float32)


def rows_to_lanes(tile):
    return jnp.sum(tile.T, axis=0, keepdims=True)


def lanes_to_rows(row):
    return jnp.broadcast_to(row, (HD, row.shape[1])).T


def square_kernel(q_ref, k_ref, out_ref):
    for i, ref in enumerate((q_ref, k_ref)):
        rows, cols = ref.shape
        total = jnp.zeros((rows, HD), jnp.float32)
        for c in range(0, cols, HD):
            x = ref[:, c : c + HD].astype(jnp.float32)
            total += x * x
        out_ref[:, i * rows : (i + 1) * rows] = rows_to_lanes(total)


def slot_of(note):
    return pl.multiple_of(((note + 1) & 1) * BLK, BLK)


BIT = 8


def is_reader(mine, notes, i):
    band, other = WAYS[i]
    note = notes[i]
    if band == 5:
        return note >= 1
    bit = mine[BIT + band]
    return (note >= 1) & ((note >= 3).astype(jnp.int32) == (1 - bit if other else bit))


def notes_kernel(place, frames, blocks, first_ref, second_ref, mine):
    half = place[1] // 2
    bands = frames.shape[1]
    for ref, band in ((first_ref, half), (second_ref, jnp.minimum(half + 4, bands - 1))):
        code = 1 + blocks[0, band] + 2 * (frames[0, band] > place[0]).astype(jnp.int32)
        ref[...] = jnp.full((1, HD), code, jnp.int32).astype(jnp.float32)
    for j in range(bands):
        mine[j] = (frames[0, j] > place[0]).astype(jnp.int32)
        mine[BIT + j] = (place[0] >> j) & 1


def norm_kernel(width, notes, sums_ref, qg_ref, kg_ref, q_ref, k_ref, v_ref, qn_ref, kn_ref, *sends):
    rows, cols = q_ref.shape
    rstd = lax.rsqrt(sums_ref[...] / width + EPS)
    q_rstd = lanes_to_rows(rstd[:, :rows])
    k_rstd = lanes_to_rows(rstd[:, rows:])
    for c in range(0, cols, HD):
        at = slice(c, c + HD)
        qn_ref[:, at] = (q_ref[:, at].astype(jnp.float32) * q_rstd * qg_ref[:, at]).astype(jnp.bfloat16)
        kn_ref[:, at] = (k_ref[:, at].astype(jnp.float32) * k_rstd * kg_ref[:, at]).astype(jnp.bfloat16)
    for i, send in enumerate(sends):
        start = slot_of(notes[i])
        send[0] = kn_ref[pl.ds(start, BLK), :]
        send[1] = v_ref[pl.ds(start, BLK), :]


def attention_kernel(width, mine, sums_ref, qg_ref, kg_ref, q_ref, k_ref, v_ref, do_ref, qpre_ref, *refs):
    recv = dict(zip(ORDER, refs[: len(WAYS)]))
    out_ref, dq_ref, dk_ref, dv_ref, inner_ref, gains_ref = refs[len(WAYS) : len(WAYS) + 6]
    parts = refs[len(WAYS) + 6 : len(WAYS) + 12]
    keys, vals = refs[len(WAYS) + 12 :]
    rows, cols = q_ref.shape
    keys[:rows] = k_ref[...]
    vals[:rows] = v_ref[...]
    for j in range(len(parts)):
        at = slice(rows + j * BLK, rows + (j + 1) * BLK)
        if j == 5:
            keys[at] = recv[j, 0][0]
            vals[at] = recv[j, 0][1]
            continue

        @pl.when(mine[j] != mine[BIT + j])
        def _(at=at, ref=recv[j, 0]):
            keys[at] = ref[0]
            vals[at] = ref[1]

        @pl.when(mine[j] == mine[BIT + j])
        def _(at=at, ref=recv[j, 1]):
            keys[at] = ref[0]
            vals[at] = ref[1]

    q_rstd = lanes_to_rows(lax.rsqrt(sums_ref[:, :rows] / width + EPS))
    inner = jnp.zeros((rows, HD), jnp.float32)
    for c in range(0, cols, HD):
        at = slice(c, c + HD)
        k = keys[:, at]
        v = vals[:, at]
        q = q_ref[:, at]
        do = do_ref[:, at]
        s = dot(k, q, ((1,), (1,)))
        top = jnp.max(s, axis=0, keepdims=True)
        e = jnp.exp2((s - top) * (SCALE * LOG2E))
        p = e * (1.0 / jnp.sum(e, axis=0, keepdims=True))
        ph = p.astype(jnp.bfloat16)
        attn_t = dot(v.T, ph, ((1,), (0,))).astype(jnp.bfloat16).astype(jnp.float32)
        out_ref[:, at] = attn_t.T.astype(jnp.bfloat16)
        delta = jnp.sum(attn_t * do.astype(jnp.float32).T, axis=0, keepdims=True)
        dp = dot(v, do, ((1,), (1,)))
        ds = (p * (dp - delta)).astype(jnp.bfloat16)
        dq = (dot(k.T, ds, ((1,), (0,))) * SCALE).T
        dq_ref[:, at] = dq
        dk = dot(ds, q, ((1,), (0,))) * SCALE
        dv = dot(ph, do, ((1,), (0,)))
        dk_ref[:, at] = dk[:rows]
        dv_ref[:, at] = dv[:rows]
        dkh = dk[rows:].astype(jnp.bfloat16)
        dvh = dv[rows:].astype(jnp.bfloat16)
        for j, part in enumerate(parts):
            part[0, :, at] = dkh[j * BLK : (j + 1) * BLK]
            part[1, :, at] = dvh[j * BLK : (j + 1) * BLK]
        pull = dq * qpre_ref[:, at].astype(jnp.float32)
        inner += pull * qg_ref[:, at]
        gains_ref[0:1, at] = jnp.sum(pull * q_rstd, axis=0, keepdims=True)
        kf = k.astype(jnp.float32)
        far = jnp.sum(dkh.astype(jnp.float32) * kf[rows:], axis=0, keepdims=True)
        own = jnp.sum(dk[:rows] * kf[:rows], axis=0, keepdims=True)
        gains_ref[1:2, at] = (far + own) / kg_ref[:, at]
    inner_ref[...] = rows_to_lanes(inner)


def collect_kernel(mine, notes, kg_ref, k_ref, *refs):
    count = 2 + len(WAYS)
    fetched = refs[:count]
    dk_out, dv_out, inner_ref, dv_sum, slots, sems = refs[count:]
    into = [dk_out, dv_sum, *(slots.at[i] for i in range(len(WAYS)))]
    copies = [pltpu.make_async_copy(ref, to, sems.at[i]) for i, (ref, to) in enumerate(zip(fetched, into, strict=True))]
    for copy in copies:
        copy.start()
    for copy in copies[:2]:
        copy.wait()
    for i in range(len(WAYS)):
        copies[2 + i].wait()

        @pl.when(is_reader(mine, notes, i))
        def _(i=i):
            at = pl.ds(slot_of(notes[i]), BLK)
            dk_out[at, :] += slots[i, 0].astype(jnp.float32)
            dv_sum[at, :] += slots[i, 1].astype(jnp.float32)

    rows, cols = dk_out.shape
    dv_out[...] = dv_sum[...].astype(jnp.bfloat16)
    inner = jnp.zeros((rows, HD), jnp.float32)
    for c in range(0, cols, HD):
        at = slice(c, c + HD)
        inner += dk_out[:, at] * kg_ref[:, at] * k_ref[:, at].astype(jnp.float32)
    inner_ref[...] = rows_to_lanes(inner)


def back_kernel(width, sums_ref, *refs):
    *refs, dq_out, dk_out = refs
    rows, cols = dq_out.shape
    for i, out in enumerate((dq_out, dk_out)):
        inner_ref, gain_ref, pre_ref, grad_ref = refs[4 * i : 4 * i + 4]
        row_rstd = lax.rsqrt(sums_ref[:, i * rows : (i + 1) * rows] / width + EPS)
        rstd = lanes_to_rows(row_rstd)
        pull = lanes_to_rows(row_rstd * row_rstd * row_rstd * (inner_ref[...] / width))
        for c in range(0, cols, HD):
            at = slice(c, c + HD)
            out[:, at] = (
                rstd * gain_ref[:, at] * grad_ref[:, at] - pre_ref[:, at].astype(jnp.float32) * pull
            ).astype(jnp.bfloat16)


def after(value, *others):
    return lax.optimization_barrier((value, *others))


VMEM = pl.BlockSpec(memory_space=pltpu.VMEM)
SMEM = pl.BlockSpec(memory_space=pltpu.SMEM)
HBM = pl.BlockSpec(memory_space=pltpu.HBM)


def call(kernel, outs, scalars, arrays, name, flops=0, limit=24, scratch=(), far=()):
    size = sum(a.size * a.dtype.itemsize for a in (*arrays, *far)) + sum(o.size * o.dtype.itemsize for o in outs)
    return pl.pallas_call(
        kernel,
        out_shape=outs,
        in_specs=[SMEM] * len(scalars) + [VMEM] * len(arrays) + [HBM] * len(far),
        out_specs=[VMEM] * len(outs),
        scratch_shapes=scratch,
        compiler_params=pltpu.CompilerParams(vmem_limit_bytes=limit * MIB),
        cost_estimate=pl.CostEstimate(flops=flops, bytes_accessed=size, transcendentals=0),
        name=name,
    )(*scalars, *arrays, *far)


def per_device(q_pre, k_pre, values, q_gain, k_gain, grad_out, far_frames, far_blocks):
    rows, cols = q_pre.shape
    width = cols * lax.axis_size("tp")
    bands = far_blocks.shape[1]
    frame = lax.axis_index(CTX)
    rank = lax.axis_index("tp")
    f32, bf16 = jnp.float32, jnp.bfloat16
    struct = jax.ShapeDtypeStruct
    q_gain, k_gain = q_gain[None], k_gain[None]

    *codes, mine = pl.pallas_call(
        notes_kernel,
        out_shape=[struct((1, HD), f32)] * 2 + [struct((16,), jnp.int32)],
        in_specs=[SMEM] * 3,
        out_specs=[VMEM] * 2 + [SMEM],
        name="notes",
    )(jnp.stack([frame, rank]), far_frames, far_blocks)
    lane = jnp.arange(HD)[None]
    notes = jnp.zeros((1, HD), f32)
    for first, code in zip((0, 8), codes):
        pairs = [(a * 8 + t, b * 8 + t) for t, d in enumerate(WAYS[first : first + 8]) for a, b in pairs_of(d)]
        got = lax.ppermute(code, (*CTX, "tp"), pairs)
        notes = notes + jnp.where(lane == first + rank, got, 0.0)
    (squares,) = call(square_kernel, [struct((1, 2 * rows), f32)], [], [q_pre, k_pre], "square")
    squares, notes = lax.psum((squares, notes), "tp")
    notes = notes[0].astype(jnp.int32)
    block = struct((2, BLK, cols), bf16)
    q_normed, k_normed, *sends = call(
        functools.partial(norm_kernel, width),
        [struct((rows, cols), bf16)] * 2 + [block] * len(WAYS),
        [notes],
        [squares, q_gain, k_gain, q_pre, k_pre, values],
        "norm",
    )
    sends = dict(zip(WAYS, sends))
    recvs = {}
    for i, d in enumerate(ORDER):
        if i >= WINDOW:
            early = ORDER[i - WINDOW]
            sends[d], recvs[early] = after(sends[d], recvs[early])
        recvs[d] = move(sends[d], d)
    recvs = [recvs[d] for d in ORDER]
    head = struct((rows, cols), f32)
    far_rows = rows + bands * BLK
    attn, dq, dk, dv, q_inner, gains, *parts = call(
        functools.partial(attention_kernel, width),
        [struct((rows, cols), bf16), head, head, head, struct((1, rows), f32), struct((2, cols), f32)] + [block] * bands,
        [mine],
        [squares, q_gain, k_gain, q_normed, k_normed, values, grad_out, q_pre, *recvs],
        "attention",
        flops=12 * rows * far_rows * cols,
        limit=32,
        scratch=[pltpu.VMEM((far_rows, cols), bf16)] * 2,
    )
    backs = [move(parts[d[0]], d) for d in WAYS]
    gains = lax.psum(lax.psum(gains, "cx"), "cy")
    dk, dv, k_inner = call(
        collect_kernel,
        [head, struct((rows, cols), bf16), struct((1, rows), f32)],
        [mine, notes],
        [k_gain, k_pre],
        "collect",
        limit=60,
        scratch=[
            pltpu.VMEM((rows, cols), f32),
            pltpu.VMEM((len(WAYS), 2, BLK, cols), bf16),
            pltpu.SemaphoreType.DMA((2 + len(WAYS),)),
        ],
        far=[dk, dv, *backs],
    )
    q_inner, k_inner = lax.psum((q_inner, k_inner), "tp")
    dq_pre, dk_pre = call(
        functools.partial(back_kernel, width),
        [struct((rows, cols), bf16)] * 2,
        [],
        [squares, q_inner, q_gain, q_pre, dq, k_inner, k_gain, k_pre, dk],
        "back",
    )
    return (attn, dq_pre, dk_pre, dv, gains[0], gains[1])


def solution(mesh):
    ctx = CTX
    split = Mesh(mesh.devices.reshape(8, 8, 8), (*CTX, "tp"))
    placed = (
        P(ctx, "tp"),
        P(ctx, "tp"),
        P(ctx, "tp"),
        P("tp"),
        P("tp"),
        P(ctx, "tp"),
        P(ctx, None),
        P(ctx, None),
    )
    return jax.shard_map(
        per_device,
        mesh=split,
        in_specs=placed,
        out_specs=(P(ctx, "tp"), P(ctx, "tp"), P(ctx, "tp"), P(ctx, "tp"), P("tp"), P("tp")),
        check_vma=False,
    )
```

time: 591 us -> 208 us (0.35)
  the two profiles are of different devices: /device:TPU:1 before, /device:TPU:8 now
where the time goes in v1:
time: 208 us; the launch traced here: 207 us
  starting transfers between devices  94.1 us (45%)
  blocking collectives  67.6 us (32%)
  Pallas kernels  17.3 us (8%)
  waiting for transfers between devices  17.1 us (8%)
  local copies, waits for them, and re-layouts  8.91 us (4%)
    ppermute x22, starting transfers between devices, move(): return lax.ppermute(value, CTX, pairs_of(way))  87.7 us
    psum x2, blocking collectives, per_device(): gains = lax.psum(lax.psum(gains, 'cx'), 'cy')  31.5 us
    psum x1, blocking collectives, per_device(): squares, notes = lax.psum((squares, notes), 'tp')  20.9 us
    ppermute x22, waiting for transfers between devices, move(): return lax.ppermute(value, CTX, pairs_of(way))  17.1 us
    pallas_call x5, Pallas kernels, call(): pl.pallas_call(kernel, out_shape=outs, in_specs=[SMEM] * len(scalars) + [...  16 us
    psum x1, blocking collectives, per_device(): q_inner, k_inner = lax.psum((q_inner, k_inner), 'tp')  15.2 us
    unnamed x50, local copies, waits for them, and re-layouts  8.29 us
    ppermute x2, starting transfers between devices, per_device(): got = lax.ppermute(code, (*CTX, 'tp'), pairs)  6.42 us
  transfers between devices with their start and end apart: 24, of which 4 were waited for; matrix products, arithmetic and copies ran while one was open for 0% of the time, Pallas kernels for 0%

profile of v1, /device:TPU:8, one launch (start us, length us, event | category | flops | bytes accessed | tf_op | source)
XLA Modules:
  0.0 206.9 jit_solution(17599928665326208081)
XLA Ops:
  0.6 0.6 pad_add_fusion.place
  1.2 1.4 notes.1
  2.6 0.0 copy-start.24
  2.6 1.9 collective-permute-start
  4.5 0.0 copy-start.22
  4.6 4.5 %collective-permute-start.1 = (f32[1,128]{1,0:T(1,128)S(1)}, f32[1,128]{1,0:T(1,128)S(1)}, u32[]{:S(2)}, u32[]{:S(2)}) collective-permute-start(f32[1,128]{1,0:T(1,128)S(1)} %copy-done.24), channel_id=1, source_target_pairs={{0,128},{128,0},{8,136},{136,8},{16,144},{144,16},{24,152},{152,24... | collective-permute-start | bytes 1544 | tf_op jit(solution)/shard_map/ppermute | solution.py:251
  9.1 0.0 copy-start
  9.1 1.0 copy-done
  10.1 1.0 copy-done.3
  11.1 0.2 square.1
  11.3 0.0 collective-permute-done.1
  11.3 20.9 %all-reduce.1 = (f32[1,512]{1,0:T(1,128)S(1)}, f32[1,128]{1,0:T(1,128)S(1)}) all-reduce(f32[1,512]{1,0:T(1,128)S(1)} %square.1, f32[1,128]{1,0:T(1,128)S(1)} %fusion), channel_id=1, replica_groups=mesh['cy'=8,'cx'=8,'tp'=8] {'tp'}, use_global_device_ids=true, to_apply=%region_0.1 | all-reduce | flops 640 | bytes 5120 | tf_op jit(solution)/shard_map/psum | solution.py:254
  32.2 0.5 copy-done.12
  32.8 1.0 copy-done.8
  33.7 1.1 norm.1
  34.9 5.7 %collective-permute-start.2 = (bf16[2,128,640]{2,1,0:T(8,128)(2,1)S(1)}, bf16[2,128,640]{2,1,0:T(8,128)(2,1)S(1)}, u32[]{:S(2)}, u32[]{:S(2)}) collective-permute-start(bf16[2,128,640]{2,1,0:T(8,128)(2,1)S(1)} %get-tuple-element.57), channel_id=1, source_target_pairs={{0,128},{128,0},{8,136},{136,8},{16,144},{144,16},{24,152},{152,24... | collective-permute-start | bytes 983048 | tf_op jit(solution)/shard_map/ppermute | solution.py:33
  40.6 0.7 collective-permute-start.3
  41.3 6.7 %collective-permute-start.4 = (bf16[2,128,640]{2,1,0:T(8,128)(2,1)S(1)}, bf16[2,128,640]{2,1,0:T(8,128)(2,1)S(1)}, u32[]{:S(2)}, u32[]{:S(2)}) collective-permute-start(bf16[2,128,640]{2,1,0:T(8,128)(2,1)S(1)} %get-tuple-element.63), channel_id=1, source_target_pairs={{0,256},{256,0},{8,264},{264,8},{16,272},{272,16},{24,280},{280,24... | collective-permute-start | bytes 983048 | tf_op jit(solution)/shard_map/ppermute | solution.py:33
  48.0 4.9 %collective-permute-start.5 = (bf16[2,128,640]{2,1,0:T(8,128)(2,1)S(1)}, bf16[2,128,640]{2,1,0:T(8,128)(2,1)S(1)}, u32[]{:S(2)}, u32[]{:S(2)}) collective-permute-start(bf16[2,128,640]{2,1,0:T(8,128)(2,1)S(1)} %get-tuple-element.66), channel_id=1, source_target_pairs={{0,32},{32,0},{8,40},{40,8},{16,48},{48,16},{24,56},{56,24},{64,96... | collective-permute-start | bytes 983048 | tf_op jit(solution)/shard_map/ppermute | solution.py:33
  52.9 1.9 collective-permute-start.6
  54.9 5.7 %collective-permute-done.2.refs_0_ = bf16[2,128,640]{2,1,0:T(8,128)(2,1)S(1)} collective-permute-done((bf16[2,128,640]{2,1,0:T(8,128)(2,1)S(1)}, bf16[2,128,640]{2,1,0:T(8,128)(2,1)S(1)}, u32[]{:S(2)}, u32[]{:S(2)}) %collective-permute-start.2) | collective-permute-done | bytes 327712 | tf_op jit(solution)/shard_map/ppermute | solution.py:33
  60.6 1.9 collective-permute-start.7
  62.5 0.0 collective-permute-done.3.refs_1_
  62.5 11.1 %collective-permute-start.8 = (bf16[2,128,640]{2,1,0:T(8,128)(2,1)S(1)}, bf16[2,128,640]{2,1,0:T(8,128)(2,1)S(1)}, u32[]{:S(2)}, u32[]{:S(2)}) collective-permute-start(bf16[2,128,640]{2,1,0:T(8,128)(2,1)S(1)} %get-tuple-element.74), channel_id=1, source_target_pairs={{64,128},{128,64},{72,136},{136,72},{80,144},{144,80},{88,152},{15... | collective-permute-start | bytes 983048 | tf_op jit(solution)/shard_map/ppermute | solution.py:33
  73.6 0.0 collective-permute-done.4.refs_2_
  73.6 3.5 %collective-permute-start.9 = (bf16[2,128,640]{2,1,0:T(8,128)(2,1)S(1)}, bf16[2,128,640]{2,1,0:T(8,128)(2,1)S(1)}, u32[]{:S(2)}, u32[]{:S(2)}) collective-permute-start(bf16[2,128,640]{2,1,0:T(8,128)(2,1)S(1)} %get-tuple-element.75), channel_id=1, source_target_pairs={{0,16},{16,0},{8,24},{24,8},{32,48},{48,32},{40,56},{56,40},{64,80... | collective-permute-start | bytes 983048 | tf_op jit(solution)/shard_map/ppermute | solution.py:33
  77.1 1.9 collective-permute-start.10
  79.0 1.9 collective-permute-start.11
  81.0 0.0 collective-permute-done.7.refs_5_
  81.0 6.1 %collective-permute-start.12 = (bf16[2,128,640]{2,1,0:T(8,128)(2,1)S(1)}, bf16[2,128,640]{2,1,0:T(8,128)(2,1)S(1)}, u32[]{:S(2)}, u32[]{:S(2)}) collective-permute-start(bf16[2,128,640]{2,1,0:T(8,128)(2,1)S(1)} %get-tuple-element.78), channel_id=1, source_target_pairs={{8,16},{16,8},{24,32},{32,24},{40,48},{48,40},{56,64},{64,56},{72,... | collective-permute-start | bytes 983048 | tf_op jit(solution)/shard_map/ppermute | solution.py:33
  87.1 0.0 collective-permute-done.9.refs_7_
  87.1 1.0 collective-permute-done.10.refs_8_
  88.2 3.7 %collective-permute-done.12.refs_10_ = bf16[2,128,640]{2,1,0:T(8,128)(2,1)S(1)} collective-permute-done((bf16[2,128,640]{2,1,0:T(8,128)(2,1)S(1)}, bf16[2,128,640]{2,1,0:T(8,128)(2,1)S(1)}, u32[]{:S(2)}, u32[]{:S(2)}) %collective-permute-start.12) | collective-permute-done | bytes 327712 | tf_op jit(solution)/shard_map/ppermute | solution.py:33
  91.9 0.6 copy-done.13
  92.5 9.1 %attention.1 = (bf16[256,640]{1,0:T(8,128)(2,1)}, f32[256,640]{1,0:T(8,128)S(1)}, f32[256,640]{1,0:T(8,128)S(1)}, f32[256,640]{1,0:T(8,128)S(1)}, f32[1,256]{1,0...) custom-call(s32[16]{0:T(128)S(1)} %copy-done.13, ...), custom_call_target="tpu_custom_call" | custom-call | flops 2013265920 | bytes 9516032 | tf_op jit(solution)/shard_map/attention/pallas_call | solution.py:218
  101.6 0.9 copy-done.6
  102.5 0.8 copy-done.7
  103.3 7.7 %collective-permute-start.23 = (bf16[2,128,640]{2,1,0:T(8,128)(2,1)S(1)}, bf16[2,128,640]{2,1,0:T(8,128)(2,1)S(1)}, u32[]{:S(2)}, u32[]{:S(2)}) collective-permute-start(bf16[2,128,640]{2,1,0:T(8,128)(2,1)S(1)} %get-tuple-element.89), channel_id=1, source_target_pairs={{0,256},{256,0},{8,264},{264,8},{16,272},{272,16},{24,280},{280,24... | collective-permute-start | bytes 983048 | tf_op jit(solution)/shard_map/ppermute | solution.py:33
  111.0 2.4 %collective-permute-start.14 = (bf16[2,128,640]{2,1,0:T(8,128)(2,1)S(1)}, bf16[2,128,640]{2,1,0:T(8,128)(2,1)S(1)}, u32[]{:S(2)}, u32[]{:S(2)}) collective-permute-start(bf16[2,128,640]{2,1,0:T(8,128)(2,1)S(1)} %get-tuple-element.84), channel_id=1, source_target_pairs={{8,16},{16,8},{24,32},{32,24},{40,48},{48,40},{56,64},{64,56},{72,... | collective-permute-start | bytes 983048 | tf_op jit(solution)/shard_map/ppermute | solution.py:33
  113.5 1.9 collective-permute-start.13
  115.4 5.6 %collective-permute-start.16 = (bf16[2,128,640]{2,1,0:T(8,128)(2,1)S(1)}, bf16[2,128,640]{2,1,0:T(8,128)(2,1)S(1)}, u32[]{:S(2)}, u32[]{:S(2)}) collective-permute-start(bf16[2,128,640]{2,1,0:T(8,128)(2,1)S(1)} %get-tuple-element.85), channel_id=1, source_target_pairs={{16,32},{32,16},{24,40},{40,24},{48,64},{64,48},{56,72},{72,56},{8... | collective-permute-start | bytes 983048 | tf_op jit(solution)/shard_map/ppermute | solution.py:33
  121.0 1.9 collective-permute-start.15
  123.0 0.0 collective-permute-done.23.refs_12_
  123.0 3.8 %collective-permute-start.18 = (bf16[2,128,640]{2,1,0:T(8,128)(2,1)S(1)}, bf16[2,128,640]{2,1,0:T(8,128)(2,1)S(1)}, u32[]{:S(2)}, u32[]{:S(2)}) collective-permute-start(bf16[2,128,640]{2,1,0:T(8,128)(2,1)S(1)} %get-tuple-element.86), channel_id=1, source_target_pairs={{32,64},{64,32},{40,72},{72,40},{48,80},{80,48},{56,88},{88,56},{9... | collective-permute-start | bytes 983048 | tf_op jit(solution)/shard_map/ppermute | solution.py:33
  126.8 6.6 %collective-permute-done.14.refs_3_ = bf16[2,128,640]{2,1,0:T(8,128)(2,1)S(1)} collective-permute-done((bf16[2,128,640]{2,1,0:T(8,128)(2,1)S(1)}, bf16[2,128,640]{2,1,0:T(8,128)(2,1)S(1)}, u32[]{:S(2)}, u32[]{:S(2)}) %collective-permute-start.14) | collective-permute-done | bytes 327712 | tf_op jit(solution)/shard_map/ppermute | solution.py:33
  133.4 1.9 collective-permute-start.17
  135.3 0.0 collective-permute-done.13.refs_2_
  135.3 0.0 copy-start.17
  135.3 5.8 %collective-permute-start.20 = (bf16[2,128,640]{2,1,0:T(8,128)(2,1)S(1)}, bf16[2,128,640]{2,1,0:T(8,128)(2,1)}, u32[]{:S(2)}, u32[]{:S(2)}) collective-permute-start(bf16[2,128,640]{2,1,0:T(8,128)(2,1)S(1)} %get-tuple-element.87), channel_id=1, source_target_pairs={{64,128},{128,64},{72,136},{136,72},{80,144},{144,80},{88,152},{15... | collective-permute-start | bytes 983048 | tf_op jit(solution)/shard_map/ppermute | solution.py:33
  141.1 0.0 collective-permute-done.16.refs_5_
  141.2 1.9 collective-permute-start.19
  143.1 0.0 collective-permute-done.15.refs_4_
  143.1 1.4 collective-permute-start.22
  144.5 6.9 %collective-permute-start.21 = (bf16[2,128,640]{2,1,0:T(8,128)(2,1)S(1)}, bf16[2,128,640]{2,1,0:T(8,128)(2,1)}, u32[]{:S(2)}, u32[]{:S(2)}) collective-permute-start(bf16[2,128,640]{2,1,0:T(8,128)(2,1)S(1)} %get-tuple-element.88), channel_id=1, source_target_pairs={{0,128},{128,0},{8,136},{136,8},{16,144},{144,16},{24,152},{152,24... | collective-permute-start | bytes 983048 | tf_op jit(solution)/shard_map/ppermute | solution.py:33
  151.5 15.5 %psum.46 = f32[2,640]{1,0:T(2,128)S(1)} all-reduce(f32[2,640]{1,0:T(2,128)S(1)} %get-tuple-element.95), channel_id=1, replica_groups=mesh['cy'=8,'cx'=8,'tp'=8] {'cx'}, use_global_device_ids=true, to_apply=%region_4.5 | all-reduce | flops 1280 | bytes 10240 | tf_op jit(solution)/shard_map/psum | solution.py:285
  166.9 16.0 %psum.47 = f32[2,640]{1,0:T(2,128)S(1)} all-reduce(f32[2,640]{1,0:T(2,128)S(1)} %psum.46), channel_id=1, replica_groups=mesh['cy'=8,'cx'=8,'tp'=8] {'cy'}, use_global_device_ids=true, to_apply=%region_5.6 | all-reduce | flops 1280 | bytes 10240 | tf_op jit(solution)/shard_map/psum | solution.py:285
  182.9 0.6 slice_reduce_fusion
  183.6 0.0 copy-start.2
  183.6 4.5 %collect.1 = (f32[256,640]{1,0:T(8,128)}, bf16[256,640]{1,0:T(8,128)(2,1)}, f32[1,256]{1,0:T(1,128)}) custom-call(s32[16]{0:T(128)} %get-tuple-element.51.mine, s32[128]{0:T(128)} %copy-done.12, f32[1,640]{1,0:T(1,128)} %copy-done.10, bf16[256,640]{1,0:T(8,128)(2,1)} %refs_6_.1, f32[256,640]{1,0:T(8,128)} %copy-done.6, f32[256,640]{1,0:T(8,128)} %copy-done.7, ...), custom_call_target="tpu_custom_call" | custom-call | bytes 6229504 | tf_op jit(solution)/shard_map/collect/pallas_call | solution.py:218
  188.2 0.7 copy-done.23
  188.8 15.2 %all-reduce = (f32[1,256]{1,0:T(1,128)S(1)}, f32[1,256]{1,0:T(1,128)S(1)}) all-reduce(f32[1,256]{1,0:T(1,128)S(1)} %get-tuple-element.80, f32[1,256]{1,0:T(1,128)S(1)} %copy-done.23), channel_id=1, replica_groups=mesh['cy'=8,'cx'=8,'tp'=8] {'tp'}, use_global_device_ids=true, to_apply=%region_2.3 | all-reduce | flops 512 | bytes 4096 | tf_op jit(solution)/shard_map/psum | solution.py:300
  204.1 0.7 copy-done.11
  204.7 1.1 copy-done.5
  205.8 1.1 back.1
  (50 shorter events, 0.1 us)
Async XLA Ops:
  1.2 7.8 %copy-start.21 = (f32[640]{0:T(1024)S(1)}, f32[640]{0:T(1024)}, u32[]{:S(2)}) copy-start(f32[640]{0:T(1024)} %param.12) | copy-start | bytes 7684
  2.6 1.9 copy-start.24
  2.6 8.7 %collective-permute-start = (f32[1,128]{1,0:T(1,128)}, f32[1,128]{1,0:T(1,128)S(1)}, u32[]{:S(2)}, u32[]{:S(2)}) collective-permute-start(f32[1,128]{1,0:T(1,128)} %get-tuple-element.52), channel_id=1, source_target_pairs={{0,8},{8,0},{16,24},{24,16},{32,40},{40,32},{48,56},{56,48},{64,72... | collective-permute-start | bytes 1544 | tf_op jit(solution)/shard_map/ppermute | solution.py:251
  4.5 4.5 %copy-start.22 = (f32[640]{0:T(1024)S(1)}, f32[640]{0:T(1024)}, u32[]{:S(2)}) copy-start(f32[640]{0:T(1024)} %param.11) | copy-start | bytes 7684
  4.6 6.7 %collective-permute-start.1 = (f32[1,128]{1,0:T(1,128)S(1)}, f32[1,128]{1,0:T(1,128)S(1)}, u32[]{:S(2)}, u32[]{:S(2)}) collective-permute-start(f32[1,128]{1,0:T(1,128)S(1)} %copy-done.24), channel_id=1, source_target_pairs={{0,128},{128,0},{8,136},{136,8},{16,144},{144,16},{24,152},{152,24... | collective-permute-start | bytes 1544 | tf_op jit(solution)/shard_map/ppermute | solution.py:251
  9.1 82.8 %copy-start.10 = (f32[1,640]{1,0:T(1,128)}, f32[1,640]{1,0:T(1,128)S(1)}, u32[]{:S(2)}) copy-start(f32[1,640]{1,0:T(1,128)S(1)} %broadcast_in_dim.13.kg_ref.refs_5_) | copy-start | bytes 7684
  9.1 1.0 copy-start
  10.1 1.0 copy-start.3
  11.1 21.7 %copy-start.1 = (bf16[256,640]{1,0:T(8,128)(2,1)S(1)}, bf16[256,640]{1,0:T(8,128)(2,1)}, u32[]{:S(2)}) copy-start(bf16[256,640]{1,0:T(8,128)(2,1)} %refs_6_.1) | copy-start | bytes 983044
  11.1 21.7 %copy-start.4 = (bf16[256,640]{1,0:T(8,128)(2,1)S(1)}, bf16[256,640]{1,0:T(8,128)(2,1)}, u32[]{:S(2)}) copy-start(bf16[256,640]{1,0:T(8,128)(2,1)} %refs_2_.1) | copy-start | bytes 983044
  32.2 0.5 copy-start.12
  32.8 1.0 copy-start.8
  33.7 58.1 %copy-start.9 = (bf16[256,640]{1,0:T(8,128)(2,1)S(1)}, bf16[256,640]{1,0:T(8,128)(2,1)}, u32[]{:S(2)}) copy-start(bf16[256,640]{1,0:T(8,128)(2,1)} %v_ref.3) | copy-start | bytes 983044
  33.7 58.1 %copy-start.14 = (bf16[256,640]{1,0:T(8,128)(2,1)S(1)}, bf16[256,640]{1,0:T(8,128)(2,1)}, u32[]{:S(2)}) copy-start(bf16[256,640]{1,0:T(8,128)(2,1)} %do_ref.1) | copy-start | bytes 983044
  34.9 25.7 %collective-permute-start.2 = (bf16[2,128,640]{2,1,0:T(8,128)(2,1)S(1)}, bf16[2,128,640]{2,1,0:T(8,128)(2,1)S(1)}, u32[]{:S(2)}, u32[]{:S(2)}) collective-permute-start(bf16[2,128,640]{2,1,0:T(8,128)(2,1)S(1)} %get-tuple-element.57), channel_id=1, source_target_pairs={{0,128},{128,0},{8,136},{136,8},{16,144},{144,16},{24,152},{152,24... | collective-permute-start | bytes 983048 | tf_op jit(solution)/shard_map/ppermute | solution.py:33
  40.6 21.9 %collective-permute-start.3 = (bf16[2,128,640]{2,1,0:T(8,128)(2,1)S(1)}, bf16[2,128,640]{2,1,0:T(8,128)(2,1)S(1)}, u32[]{:S(2)}, u32[]{:S(2)}) collective-permute-start(bf16[2,128,640]{2,1,0:T(8,128)(2,1)S(1)} %get-tuple-element.60), channel_id=1, source_target_pairs={{128,256},{256,128},{136,264},{264,136},{144,272},{272,144},{152,2... | collective-permute-start | bytes 983048 | tf_op jit(solution)/shard_map/ppermute | solution.py:33
  41.3 32.3 %collective-permute-start.4 = (bf16[2,128,640]{2,1,0:T(8,128)(2,1)S(1)}, bf16[2,128,640]{2,1,0:T(8,128)(2,1)S(1)}, u32[]{:S(2)}, u32[]{:S(2)}) collective-permute-start(bf16[2,128,640]{2,1,0:T(8,128)(2,1)S(1)} %get-tuple-element.63), channel_id=1, source_target_pairs={{0,256},{256,0},{8,264},{264,8},{16,272},{272,16},{24,280},{280,24... | collective-permute-start | bytes 983048 | tf_op jit(solution)/shard_map/ppermute | solution.py:33
  48.0 29.1 %collective-permute-start.5 = (bf16[2,128,640]{2,1,0:T(8,128)(2,1)S(1)}, bf16[2,128,640]{2,1,0:T(8,128)(2,1)S(1)}, u32[]{:S(2)}, u32[]{:S(2)}) collective-permute-start(bf16[2,128,640]{2,1,0:T(8,128)(2,1)S(1)} %get-tuple-element.66), channel_id=1, source_target_pairs={{0,32},{32,0},{8,40},{40,8},{16,48},{48,16},{24,56},{56,24},{64,96... | collective-permute-start | bytes 983048 | tf_op jit(solution)/shard_map/ppermute | solution.py:33
  52.9 26.1 %collective-permute-start.6 = (bf16[2,128,640]{2,1,0:T(8,128)(2,1)S(1)}, bf16[2,128,640]{2,1,0:T(8,128)(2,1)S(1)}, u32[]{:S(2)}, u32[]{:S(2)}) collective-permute-start(bf16[2,128,640]{2,1,0:T(8,128)(2,1)S(1)} %get-tuple-element.69), channel_id=1, source_target_pairs={{32,64},{64,32},{40,72},{72,40},{48,80},{80,48},{56,88},{88,56},{9... | collective-permute-start | bytes 983048 | tf_op jit(solution)/shard_map/ppermute | solution.py:33
  60.6 20.4 %collective-permute-start.7 = (bf16[2,128,640]{2,1,0:T(8,128)(2,1)S(1)}, bf16[2,128,640]{2,1,0:T(8,128)(2,1)S(1)}, u32[]{:S(2)}, u32[]{:S(2)}) collective-permute-start(bf16[2,128,640]{2,1,0:T(8,128)(2,1)S(1)} %get-tuple-element.72), channel_id=1, source_target_pairs={{0,64},{64,0},{8,72},{72,8},{16,80},{80,16},{24,88},{88,24},{32,96... | collective-permute-start | bytes 983048 | tf_op jit(solution)/shard_map/ppermute | solution.py:33
  62.5 24.6 %collective-permute-start.8 = (bf16[2,128,640]{2,1,0:T(8,128)(2,1)S(1)}, bf16[2,128,640]{2,1,0:T(8,128)(2,1)S(1)}, u32[]{:S(2)}, u32[]{:S(2)}) collective-permute-start(bf16[2,128,640]{2,1,0:T(8,128)(2,1)S(1)} %get-tuple-element.74), channel_id=1, source_target_pairs={{64,128},{128,64},{72,136},{136,72},{80,144},{144,80},{88,152},{15... | collective-permute-start | bytes 983048 | tf_op jit(solution)/shard_map/ppermute | solution.py:33
  73.6 13.5 %collective-permute-start.9 = (bf16[2,128,640]{2,1,0:T(8,128)(2,1)S(1)}, bf16[2,128,640]{2,1,0:T(8,128)(2,1)S(1)}, u32[]{:S(2)}, u32[]{:S(2)}) collective-permute-start(bf16[2,128,640]{2,1,0:T(8,128)(2,1)S(1)} %get-tuple-element.75), channel_id=1, source_target_pairs={{0,16},{16,0},{8,24},{24,8},{32,48},{48,32},{40,56},{56,40},{64,80... | collective-permute-start | bytes 983048 | tf_op jit(solution)/shard_map/ppermute | solution.py:33
  77.1 11.1 %collective-permute-start.10 = (bf16[2,128,640]{2,1,0:T(8,128)(2,1)S(1)}, bf16[2,128,640]{2,1,0:T(8,128)(2,1)S(1)}, u32[]{:S(2)}, u32[]{:S(2)}) collective-permute-start(bf16[2,128,640]{2,1,0:T(8,128)(2,1)S(1)} %get-tuple-element.76), channel_id=1, source_target_pairs={{16,32},{32,16},{24,40},{40,24},{48,64},{64,48},{56,72},{72,56},{8... | collective-permute-start | bytes 983048 | tf_op jit(solution)/shard_map/ppermute | solution.py:33
  79.0 9.1 %collective-permute-start.11 = (bf16[2,128,640]{2,1,0:T(8,128)(2,1)S(1)}, bf16[2,128,640]{2,1,0:T(8,128)(2,1)S(1)}, u32[]{:S(2)}, u32[]{:S(2)}) collective-permute-start(bf16[2,128,640]{2,1,0:T(8,128)(2,1)S(1)} %get-tuple-element.77), channel_id=1, source_target_pairs={{0,8},{8,0},{16,24},{24,16},{32,40},{40,32},{48,56},{56,48},{64,72... | collective-permute-start | bytes 983048 | tf_op jit(solution)/shard_map/ppermute | solution.py:33
  81.0 10.9 %collective-permute-start.12 = (bf16[2,128,640]{2,1,0:T(8,128)(2,1)S(1)}, bf16[2,128,640]{2,1,0:T(8,128)(2,1)S(1)}, u32[]{:S(2)}, u32[]{:S(2)}) collective-permute-start(bf16[2,128,640]{2,1,0:T(8,128)(2,1)S(1)} %get-tuple-element.78), channel_id=1, source_target_pairs={{8,16},{16,8},{24,32},{32,24},{40,48},{48,40},{56,64},{64,56},{72,... | collective-permute-start | bytes 983048 | tf_op jit(solution)/shard_map/ppermute | solution.py:33
  91.9 0.7 copy-start.13
  101.6 0.9 copy-start.6
  102.5 0.8 copy-start.7
  103.3 19.6 %collective-permute-start.23 = (bf16[2,128,640]{2,1,0:T(8,128)(2,1)S(1)}, bf16[2,128,640]{2,1,0:T(8,128)(2,1)S(1)}, u32[]{:S(2)}, u32[]{:S(2)}) collective-permute-start(bf16[2,128,640]{2,1,0:T(8,128)(2,1)S(1)} %get-tuple-element.89), channel_id=1, source_target_pairs={{0,256},{256,0},{8,264},{264,8},{16,272},{272,16},{24,280},{280,24... | collective-permute-start | bytes 983048 | tf_op jit(solution)/shard_map/ppermute | solution.py:33
  111.0 22.3 %collective-permute-start.14 = (bf16[2,128,640]{2,1,0:T(8,128)(2,1)S(1)}, bf16[2,128,640]{2,1,0:T(8,128)(2,1)S(1)}, u32[]{:S(2)}, u32[]{:S(2)}) collective-permute-start(bf16[2,128,640]{2,1,0:T(8,128)(2,1)S(1)} %get-tuple-element.84), channel_id=1, source_target_pairs={{8,16},{16,8},{24,32},{32,24},{40,48},{48,40},{56,64},{64,56},{72,... | collective-permute-start | bytes 983048 | tf_op jit(solution)/shard_map/ppermute | solution.py:33
  113.5 21.8 %collective-permute-start.13 = (bf16[2,128,640]{2,1,0:T(8,128)(2,1)S(1)}, bf16[2,128,640]{2,1,0:T(8,128)(2,1)S(1)}, u32[]{:S(2)}, u32[]{:S(2)}) collective-permute-start(bf16[2,128,640]{2,1,0:T(8,128)(2,1)S(1)} %get-tuple-element.84), channel_id=1, source_target_pairs={{0,8},{8,0},{16,24},{24,16},{32,40},{40,32},{48,56},{56,48},{64,72... | collective-permute-start | bytes 983048 | tf_op jit(solution)/shard_map/ppermute | solution.py:33
  115.4 25.7 %collective-permute-start.16 = (bf16[2,128,640]{2,1,0:T(8,128)(2,1)S(1)}, bf16[2,128,640]{2,1,0:T(8,128)(2,1)S(1)}, u32[]{:S(2)}, u32[]{:S(2)}) collective-permute-start(bf16[2,128,640]{2,1,0:T(8,128)(2,1)S(1)} %get-tuple-element.85), channel_id=1, source_target_pairs={{16,32},{32,16},{24,40},{40,24},{48,64},{64,48},{56,72},{72,56},{8... | collective-permute-start | bytes 983048 | tf_op jit(solution)/shard_map/ppermute | solution.py:33
  121.0 22.1 %collective-permute-start.15 = (bf16[2,128,640]{2,1,0:T(8,128)(2,1)S(1)}, bf16[2,128,640]{2,1,0:T(8,128)(2,1)S(1)}, u32[]{:S(2)}, u32[]{:S(2)}) collective-permute-start(bf16[2,128,640]{2,1,0:T(8,128)(2,1)S(1)} %get-tuple-element.85), channel_id=1, source_target_pairs={{0,16},{16,0},{8,24},{24,8},{32,48},{48,32},{40,56},{56,40},{64,80... | collective-permute-start | bytes 983048 | tf_op jit(solution)/shard_map/ppermute | solution.py:33
  123.0 60.6 %copy-start.15 = (bf16[2,128,640]{2,1,0:T(8,128)(2,1)}, bf16[2,128,640]{2,1,0:T(8,128)(2,1)S(1)}, u32[]{:S(2)}) copy-start(bf16[2,128,640]{2,1,0:T(8,128)(2,1)S(1)} %collective-permute-done.23.refs_12_) | copy-start | bytes 983044
  123.0 21.5 %collective-permute-start.18 = (bf16[2,128,640]{2,1,0:T(8,128)(2,1)S(1)}, bf16[2,128,640]{2,1,0:T(8,128)(2,1)S(1)}, u32[]{:S(2)}, u32[]{:S(2)}) collective-permute-start(bf16[2,128,640]{2,1,0:T(8,128)(2,1)S(1)} %get-tuple-element.86), channel_id=1, source_target_pairs={{32,64},{64,32},{40,72},{72,40},{48,80},{80,48},{56,88},{88,56},{9... | collective-permute-start | bytes 983048 | tf_op jit(solution)/shard_map/ppermute | solution.py:33
  133.4 50.2 %copy-start.16 = (bf16[2,128,640]{2,1,0:T(8,128)(2,1)}, bf16[2,128,640]{2,1,0:T(8,128)(2,1)S(1)}, u32[]{:S(2)}) copy-start(bf16[2,128,640]{2,1,0:T(8,128)(2,1)S(1)} %collective-permute-done.14.refs_3_) | copy-start | bytes 983044
  133.4 50.2 %collective-permute-start.17 = (bf16[2,128,640]{2,1,0:T(8,128)(2,1)S(1)}, bf16[2,128,640]{2,1,0:T(8,128)(2,1)}, u32[]{:S(2)}, u32[]{:S(2)}) collective-permute-start(bf16[2,128,640]{2,1,0:T(8,128)(2,1)S(1)} %get-tuple-element.86), channel_id=1, source_target_pairs={{0,32},{32,0},{8,40},{40,8},{16,48},{48,16},{24,56},{56,24},{64,96... | collective-permute-start | bytes 983048 | tf_op jit(solution)/shard_map/ppermute | solution.py:33
  135.3 48.3 %copy-start.17 = (bf16[2,128,640]{2,1,0:T(8,128)(2,1)}, bf16[2,128,640]{2,1,0:T(8,128)(2,1)S(1)}, u32[]{:S(2)}) copy-start(bf16[2,128,640]{2,1,0:T(8,128)(2,1)S(1)} %collective-permute-done.13.refs_2_) | copy-start | bytes 983044
  135.3 48.3 %collective-permute-start.20 = (bf16[2,128,640]{2,1,0:T(8,128)(2,1)S(1)}, bf16[2,128,640]{2,1,0:T(8,128)(2,1)}, u32[]{:S(2)}, u32[]{:S(2)}) collective-permute-start(bf16[2,128,640]{2,1,0:T(8,128)(2,1)S(1)} %get-tuple-element.87), channel_id=1, source_target_pairs={{64,128},{128,64},{72,136},{136,72},{80,144},{144,80},{88,152},{15... | collective-permute-start | bytes 983048 | tf_op jit(solution)/shard_map/ppermute | solution.py:33
  141.2 10.3 %copy-start.18 = (bf16[2,128,640]{2,1,0:T(8,128)(2,1)}, bf16[2,128,640]{2,1,0:T(8,128)(2,1)S(1)}, u32[]{:S(2)}) copy-start(bf16[2,128,640]{2,1,0:T(8,128)(2,1)S(1)} %collective-permute-done.16.refs_5_) | copy-start | bytes 983044
  141.2 42.4 %collective-permute-start.19 = (bf16[2,128,640]{2,1,0:T(8,128)(2,1)S(1)}, bf16[2,128,640]{2,1,0:T(8,128)(2,1)}, u32[]{:S(2)}, u32[]{:S(2)}) collective-permute-start(bf16[2,128,640]{2,1,0:T(8,128)(2,1)S(1)} %get-tuple-element.87), channel_id=1, source_target_pairs={{0,64},{64,0},{8,72},{72,8},{16,80},{80,16},{24,88},{88,24},{32,96... | collective-permute-start | bytes 983048 | tf_op jit(solution)/shard_map/ppermute | solution.py:33
  143.1 8.3 %copy-start.19 = (bf16[2,128,640]{2,1,0:T(8,128)(2,1)}, bf16[2,128,640]{2,1,0:T(8,128)(2,1)S(1)}, u32[]{:S(2)}) copy-start(bf16[2,128,640]{2,1,0:T(8,128)(2,1)S(1)} %collective-permute-done.15.refs_4_) | copy-start | bytes 983044
  143.1 40.5 %collective-permute-start.22 = (bf16[2,128,640]{2,1,0:T(8,128)(2,1)S(1)}, bf16[2,128,640]{2,1,0:T(8,128)(2,1)}, u32[]{:S(2)}, u32[]{:S(2)}) collective-permute-start(bf16[2,128,640]{2,1,0:T(8,128)(2,1)S(1)} %get-tuple-element.88), channel_id=1, source_target_pairs={{128,256},{256,128},{136,264},{264,136},{144,272},{272,144},{152,2... | collective-permute-start | bytes 983048 | tf_op jit(solution)/shard_map/ppermute | solution.py:33
  144.5 6.9 %copy-start.20 = (bf16[2,128,640]{2,1,0:T(8,128)(2,1)}, bf16[2,128,640]{2,1,0:T(8,128)(2,1)S(1)}, u32[]{:S(2)}) copy-start(bf16[2,128,640]{2,1,0:T(8,128)(2,1)S(1)} %collective-permute-done.18.refs_7_) | copy-start | bytes 983044
  144.5 39.1 %collective-permute-start.21 = (bf16[2,128,640]{2,1,0:T(8,128)(2,1)S(1)}, bf16[2,128,640]{2,1,0:T(8,128)(2,1)}, u32[]{:S(2)}, u32[]{:S(2)}) collective-permute-start(bf16[2,128,640]{2,1,0:T(8,128)(2,1)S(1)} %get-tuple-element.88), channel_id=1, source_target_pairs={{0,128},{128,0},{8,136},{136,8},{16,144},{144,16},{24,152},{152,24... | collective-permute-start | bytes 983048 | tf_op jit(solution)/shard_map/ppermute | solution.py:33
  183.6 20.5 %copy-start.2 = (bf16[256,640]{1,0:T(8,128)(2,1)S(1)}, bf16[256,640]{1,0:T(8,128)(2,1)}, u32[]{:S(2)}) copy-start(bf16[256,640]{1,0:T(8,128)(2,1)} %refs_6_.1) | copy-start | bytes 983044
  188.2 0.7 copy-start.23
  204.1 0.7 copy-start.11
  204.7 1.1 copy-start.5

commit v2 on v1

--- a/solution.py
+++ b/solution.py
@@ -135,12 +135,12 @@
         e = jnp.exp2((s - top) * (SCALE * LOG2E))
         p = e * (1.0 / jnp.sum(e, axis=0, keepdims=True))
         ph = p.astype(jnp.bfloat16)
-        attn_t = dot(v.T, ph, ((1,), (0,))).astype(jnp.bfloat16).astype(jnp.float32)
+        attn_t = dot(v, ph, ((0,), (0,))).astype(jnp.bfloat16).astype(jnp.float32)
         out_ref[:, at] = attn_t.T.astype(jnp.bfloat16)
         delta = jnp.sum(attn_t * do.astype(jnp.float32).T, axis=0, keepdims=True)
         dp = dot(v, do, ((1,), (1,)))
         ds = (p * (dp - delta)).astype(jnp.bfloat16)
-        dq = (dot(k.T, ds, ((1,), (0,))) * SCALE).T
+        dq = (dot(k, ds, ((0,), (0,))) * SCALE).T
         dq_ref[:, at] = dq
         dk = dot(ds, q, ((1,), (0,))) * SCALE
         dv = dot(ph, do, ((1,), (0,)))
@@ -278,7 +278,7 @@
         [squares, q_gain, k_gain, q_normed, k_normed, values, grad_out, q_pre, *recvs],
         "attention",
         flops=12 * rows * far_rows * cols,
-        limit=32,
+        limit=46,
         scratch=[pltpu.VMEM((far_rows, cols), bf16)] * 2,
     )
     backs = [move(parts[d[0]], d) for d in WAYS]

time: 208 us -> 207 us (level)
    unnamed x50 -> x46, local copies, waits for them, and re-layouts: 8.29 us -> 6.56 us
where the time goes in v2:
time: 207 us; the launch traced here: 206 us
  starting transfers between devices  94 us (45%)
  blocking collectives  67.6 us (33%)
  Pallas kernels  17.7 us (9%)
  waiting for transfers between devices  17.2 us (8%)
  local copies, waits for them, and re-layouts  7.18 us (3%)
    ppermute x22, starting transfers between devices, move(): return lax.ppermute(value, CTX, pairs_of(way))  87.6 us
    psum x2, blocking collectives, per_device(): gains = lax.psum(lax.psum(gains, 'cx'), 'cy')  31.5 us
    psum x1, blocking collectives, per_device(): squares, notes = lax.psum((squares, notes), 'tp')  20.9 us
    ppermute x22, waiting for transfers between devices, move(): return lax.ppermute(value, CTX, pairs_of(way))  17.2 us
    pallas_call x5, Pallas kernels, call(): pl.pallas_call(kernel, out_shape=outs, in_specs=[SMEM] * len(scalars) + [...  16.3 us
    psum x1, blocking collectives, per_device(): q_inner, k_inner = lax.psum((q_inner, k_inner), 'tp')  15.2 us
    unnamed x46, local copies, waits for them, and re-layouts  6.56 us
    ppermute x2, starting transfers between devices, per_device(): got = lax.ppermute(code, (*CTX, 'tp'), pairs)  6.42 us
  transfers between devices with their start and end apart: 24, of which 4 were waited for; matrix products, arithmetic and copies ran while one was open for 0% of the time, Pallas kernels for 0%

profile of v2, /device:TPU:8, one launch (start us, length us, event | category | flops | bytes accessed | tf_op | source)
XLA Modules:
  0.0 205.5 jit_solution(12582221965154689378)
XLA Ops:
  0.6 0.6 pad_add_fusion.place
  1.2 1.4 notes.1
  2.6 0.0 copy-start.22
  2.6 1.9 collective-permute-start
  4.5 0.0 copy-start.20
  4.6 4.5 %collective-permute-start.1 = (f32[1,128]{1,0:T(1,128)S(1)}, f32[1,128]{1,0:T(1,128)S(1)}, u32[]{:S(2)}, u32[]{:S(2)}) collective-permute-start(f32[1,128]{1,0:T(1,128)S(1)} %copy-done.22), channel_id=1, source_target_pairs={{0,128},{128,0},{8,136},{136,8},{16,144},{144,16},{24,152},{152,24... | collective-permute-start | bytes 1544 | tf_op jit(solution)/shard_map/ppermute | solution.py:251
  9.1 0.0 copy-start
  9.1 1.0 copy-done
  10.1 1.0 copy-done.3
  11.1 0.2 square.1
  11.3 0.0 collective-permute-done
  11.3 0.0 collective-permute-done.1
  11.3 20.9 %all-reduce.1 = (f32[1,512]{1,0:T(1,128)S(1)}, f32[1,128]{1,0:T(1,128)S(1)}) all-reduce(f32[1,512]{1,0:T(1,128)S(1)} %square.1, f32[1,128]{1,0:T(1,128)S(1)} %fusion), channel_id=1, replica_groups=mesh['cy'=8,'cx'=8,'tp'=8] {'tp'}, use_global_device_ids=true, to_apply=%region_0.1 | all-reduce | flops 640 | bytes 5120 | tf_op jit(solution)/shard_map/psum | solution.py:254
  32.2 0.5 copy-done.10
  32.7 1.0 copy-done.6
  33.7 1.1 norm.1
  34.9 5.7 %collective-permute-start.2 = (bf16[2,128,640]{2,1,0:T(8,128)(2,1)S(1)}, bf16[2,128,640]{2,1,0:T(8,128)(2,1)S(1)}, u32[]{:S(2)}, u32[]{:S(2)}) collective-permute-start(bf16[2,128,640]{2,1,0:T(8,128)(2,1)S(1)} %get-tuple-element.57), channel_id=1, source_target_pairs={{0,128},{128,0},{8,136},{136,8},{16,144},{144,16},{24,152},{152,24... | collective-permute-start | bytes 983048 | tf_op jit(solution)/shard_map/ppermute | solution.py:33
  40.6 0.7 collective-permute-start.3
  41.3 6.7 %collective-permute-start.4 = (bf16[2,128,640]{2,1,0:T(8,128)(2,1)S(1)}, bf16[2,128,640]{2,1,0:T(8,128)(2,1)S(1)}, u32[]{:S(2)}, u32[]{:S(2)}) collective-permute-start(bf16[2,128,640]{2,1,0:T(8,128)(2,1)S(1)} %get-tuple-element.63), channel_id=1, source_target_pairs={{0,256},{256,0},{8,264},{264,8},{16,272},{272,16},{24,280},{280,24... | collective-permute-start | bytes 983048 | tf_op jit(solution)/shard_map/ppermute | solution.py:33
  48.0 4.9 %collective-permute-start.5 = (bf16[2,128,640]{2,1,0:T(8,128)(2,1)S(1)}, bf16[2,128,640]{2,1,0:T(8,128)(2,1)S(1)}, u32[]{:S(2)}, u32[]{:S(2)}) collective-permute-start(bf16[2,128,640]{2,1,0:T(8,128)(2,1)S(1)} %get-tuple-element.66), channel_id=1, source_target_pairs={{0,32},{32,0},{8,40},{40,8},{16,48},{48,16},{24,56},{56,24},{64,96... | collective-permute-start | bytes 983048 | tf_op jit(solution)/shard_map/ppermute | solution.py:33
  52.9 1.9 collective-permute-start.6
  54.9 5.7 %collective-permute-done.2.refs_0_ = bf16[2,128,640]{2,1,0:T(8,128)(2,1)S(1)} collective-permute-done((bf16[2,128,640]{2,1,0:T(8,128)(2,1)S(1)}, bf16[2,128,640]{2,1,0:T(8,128)(2,1)S(1)}, u32[]{:S(2)}, u32[]{:S(2)}) %collective-permute-start.2) | collective-permute-done | bytes 327712 | tf_op jit(solution)/shard_map/ppermute | solution.py:33
  60.6 1.9 collective-permute-start.7
  62.5 11.1 %collective-permute-start.8 = (bf16[2,128,640]{2,1,0:T(8,128)(2,1)S(1)}, bf16[2,128,640]{2,1,0:T(8,128)(2,1)S(1)}, u32[]{:S(2)}, u32[]{:S(2)}) collective-permute-start(bf16[2,128,640]{2,1,0:T(8,128)(2,1)S(1)} %get-tuple-element.74), channel_id=1, source_target_pairs={{64,128},{128,64},{72,136},{136,72},{80,144},{144,80},{88,152},{15... | collective-permute-start | bytes 983048 | tf_op jit(solution)/shard_map/ppermute | solution.py:33
  73.6 0.0 collective-permute-done.4.refs_2_
  73.6 3.5 %collective-permute-start.9 = (bf16[2,128,640]{2,1,0:T(8,128)(2,1)S(1)}, bf16[2,128,640]{2,1,0:T(8,128)(2,1)S(1)}, u32[]{:S(2)}, u32[]{:S(2)}) collective-permute-start(bf16[2,128,640]{2,1,0:T(8,128)(2,1)S(1)} %get-tuple-element.75), channel_id=1, source_target_pairs={{0,16},{16,0},{8,24},{24,8},{32,48},{48,32},{40,56},{56,40},{64,80... | collective-permute-start | bytes 983048 | tf_op jit(solution)/shard_map/ppermute | solution.py:33
  77.1 0.0 collective-permute-done.5.refs_3_
  77.1 1.9 collective-permute-start.10
  79.0 1.9 collective-permute-start.11
  81.0 0.0 collective-permute-done.7.refs_5_
  81.0 6.1 %collective-permute-start.12 = (bf16[2,128,640]{2,1,0:T(8,128)(2,1)S(1)}, bf16[2,128,640]{2,1,0:T(8,128)(2,1)S(1)}, u32[]{:S(2)}, u32[]{:S(2)}) collective-permute-start(bf16[2,128,640]{2,1,0:T(8,128)(2,1)S(1)} %get-tuple-element.78), channel_id=1, source_target_pairs={{8,16},{16,8},{24,32},{32,24},{40,48},{48,40},{56,64},{64,56},{72,... | collective-permute-start | bytes 983048 | tf_op jit(solution)/shard_map/ppermute | solution.py:33
  87.1 0.0 collective-permute-done.9.refs_7_
  87.1 1.0 collective-permute-done.10.refs_8_
  88.2 3.7 %collective-permute-done.12.refs_10_ = bf16[2,128,640]{2,1,0:T(8,128)(2,1)S(1)} collective-permute-done((bf16[2,128,640]{2,1,0:T(8,128)(2,1)S(1)}, bf16[2,128,640]{2,1,0:T(8,128)(2,1)S(1)}, u32[]{:S(2)}, u32[]{:S(2)}) %collective-permute-start.12) | collective-permute-done | bytes 327712 | tf_op jit(solution)/shard_map/ppermute | solution.py:33
  91.9 0.7 copy-done.11
  92.5 9.4 %attention.1 = (bf16[256,640]{1,0:T(8,128)(2,1)}, f32[256,640]{1,0:T(8,128)S(1)}, f32[256,640]{1,0:T(8,128)}, f32[256,640]{1,0:T(8,128)}, f32[1,256]{1,0:T(1,128...) custom-call(s32[16]{0:T(128)S(1)} %copy-done.11, ...), custom_call_target="tpu_custom_call" | custom-call | flops 2013265920 | bytes 9516032 | tf_op jit(solution)/shard_map/attention/pallas_call | solution.py:218
  101.9 7.7 %collective-permute-start.23 = (bf16[2,128,640]{2,1,0:T(8,128)(2,1)S(1)}, bf16[2,128,640]{2,1,0:T(8,128)(2,1)S(1)}, u32[]{:S(2)}, u32[]{:S(2)}) collective-permute-start(bf16[2,128,640]{2,1,0:T(8,128)(2,1)S(1)} %get-tuple-element.89), channel_id=1, source_target_pairs={{0,256},{256,0},{8,264},{264,8},{16,272},{272,16},{24,280},{280,24... | collective-permute-start | bytes 983048 | tf_op jit(solution)/shard_map/ppermute | solution.py:33
  109.7 2.4 %collective-permute-start.14 = (bf16[2,128,640]{2,1,0:T(8,128)(2,1)S(1)}, bf16[2,128,640]{2,1,0:T(8,128)(2,1)S(1)}, u32[]{:S(2)}, u32[]{:S(2)}) collective-permute-start(bf16[2,128,640]{2,1,0:T(8,128)(2,1)S(1)} %get-tuple-element.84), channel_id=1, source_target_pairs={{8,16},{16,8},{24,32},{32,24},{40,48},{48,40},{56,64},{64,56},{72,... | collective-permute-start | bytes 983048 | tf_op jit(solution)/shard_map/ppermute | solution.py:33
  112.1 1.9 collective-permute-start.13
  114.0 5.6 %collective-permute-start.16 = (bf16[2,128,640]{2,1,0:T(8,128)(2,1)S(1)}, bf16[2,128,640]{2,1,0:T(8,128)(2,1)S(1)}, u32[]{:S(2)}, u32[]{:S(2)}) collective-permute-start(bf16[2,128,640]{2,1,0:T(8,128)(2,1)S(1)} %get-tuple-element.85), channel_id=1, source_target_pairs={{16,32},{32,16},{24,40},{40,24},{48,64},{64,48},{56,72},{72,56},{8... | collective-permute-start | bytes 983048 | tf_op jit(solution)/shard_map/ppermute | solution.py:33
  119.7 1.9 collective-permute-start.15
  121.6 0.0 collective-permute-done.23.refs_12_
  121.6 3.8 %collective-permute-start.18 = (bf16[2,128,640]{2,1,0:T(8,128)(2,1)S(1)}, bf16[2,128,640]{2,1,0:T(8,128)(2,1)S(1)}, u32[]{:S(2)}, u32[]{:S(2)}) collective-permute-start(bf16[2,128,640]{2,1,0:T(8,128)(2,1)S(1)} %get-tuple-element.86), channel_id=1, source_target_pairs={{32,64},{64,32},{40,72},{72,40},{48,80},{80,48},{56,88},{88,56},{9... | collective-permute-start | bytes 983048 | tf_op jit(solution)/shard_map/ppermute | solution.py:33
  125.4 6.7 %collective-permute-done.14.refs_3_ = bf16[2,128,640]{2,1,0:T(8,128)(2,1)S(1)} collective-permute-done((bf16[2,128,640]{2,1,0:T(8,128)(2,1)S(1)}, bf16[2,128,640]{2,1,0:T(8,128)(2,1)S(1)}, u32[]{:S(2)}, u32[]{:S(2)}) %collective-permute-start.14) | collective-permute-done | bytes 327712 | tf_op jit(solution)/shard_map/ppermute | solution.py:33
  132.1 1.9 collective-permute-start.17
  134.0 0.0 collective-permute-done.13.refs_2_
  134.0 0.0 copy-start.15
  134.0 5.8 %collective-permute-start.20 = (bf16[2,128,640]{2,1,0:T(8,128)(2,1)S(1)}, bf16[2,128,640]{2,1,0:T(8,128)(2,1)}, u32[]{:S(2)}, u32[]{:S(2)}) collective-permute-start(bf16[2,128,640]{2,1,0:T(8,128)(2,1)S(1)} %get-tuple-element.87), channel_id=1, source_target_pairs={{64,128},{128,64},{72,136},{136,72},{80,144},{144,80},{88,152},{15... | collective-permute-start | bytes 983048 | tf_op jit(solution)/shard_map/ppermute | solution.py:33
  139.9 1.9 collective-permute-start.19
  141.8 1.4 collective-permute-start.22
  143.2 6.8 %collective-permute-start.21 = (bf16[2,128,640]{2,1,0:T(8,128)(2,1)S(1)}, bf16[2,128,640]{2,1,0:T(8,128)(2,1)}, u32[]{:S(2)}, u32[]{:S(2)}) collective-permute-start(bf16[2,128,640]{2,1,0:T(8,128)(2,1)S(1)} %get-tuple-element.88), channel_id=1, source_target_pairs={{0,128},{128,0},{8,136},{136,8},{16,144},{144,16},{24,152},{152,24... | collective-permute-start | bytes 983048 | tf_op jit(solution)/shard_map/ppermute | solution.py:33
  150.1 15.5 %psum.46 = f32[2,640]{1,0:T(2,128)S(1)} all-reduce(f32[2,640]{1,0:T(2,128)S(1)} %get-tuple-element.95), channel_id=1, replica_groups=mesh['cy'=8,'cx'=8,'tp'=8] {'cx'}, use_global_device_ids=true, to_apply=%region_4.5 | all-reduce | flops 1280 | bytes 10240 | tf_op jit(solution)/shard_map/psum | solution.py:285
  165.6 16.0 %psum.47 = f32[2,640]{1,0:T(2,128)S(1)} all-reduce(f32[2,640]{1,0:T(2,128)S(1)} %psum.46), channel_id=1, replica_groups=mesh['cy'=8,'cx'=8,'tp'=8] {'cy'}, use_global_device_ids=true, to_apply=%region_5.6 | all-reduce | flops 1280 | bytes 10240 | tf_op jit(solution)/shard_map/psum | solution.py:285
  181.6 0.6 slice_reduce_fusion
  182.2 0.0 collective-permute-done.20.refs_9_
  182.2 0.0 collective-permute-done.19.refs_8_
  182.2 0.0 collective-permute-done.21.refs_10_
  182.3 0.0 copy-start.2
  182.3 4.5 %collect.1 = (f32[256,640]{1,0:T(8,128)}, bf16[256,640]{1,0:T(8,128)(2,1)}, f32[1,256]{1,0:T(1,128)}) custom-call(s32[16]{0:T(128)} %get-tuple-element.51.mine, s32[128]{0:T(128)} %copy-done.10, f32[1,640]{1,0:T(1,128)} %copy-done.8, bf16[256,640]{1,0:T(8,128)(2,1)} %refs_6_.1, f32[256,640]{1,0:T(8,128)} %get-tuple-element.82.refs_0_, ...), custom_call_target="tpu_custom_call" | custom-call | bytes 6229504 | tf_op jit(solution)/shard_map/collect/pallas_call | solution.py:218
  186.8 0.6 copy-done.21
  187.4 15.2 %all-reduce = (f32[1,256]{1,0:T(1,128)S(1)}, f32[1,256]{1,0:T(1,128)S(1)}) all-reduce(f32[1,256]{1,0:T(1,128)S(1)} %get-tuple-element.80, f32[1,256]{1,0:T(1,128)S(1)} %copy-done.21), channel_id=1, replica_groups=mesh['cy'=8,'cx'=8,'tp'=8] {'tp'}, use_global_device_ids=true, to_apply=%region_2.3 | all-reduce | flops 512 | bytes 4096 | tf_op jit(solution)/shard_map/psum | solution.py:300
  202.7 0.7 copy-done.9
  203.3 1.1 copy-done.5
  204.4 1.1 back.1
  (46 shorter events, 0.1 us)
Async XLA Ops:
  1.2 7.8 %copy-start.19 = (f32[640]{0:T(1024)S(1)}, f32[640]{0:T(1024)}, u32[]{:S(2)}) copy-start(f32[640]{0:T(1024)} %param.12) | copy-start | bytes 7684
  2.6 1.9 copy-start.22
  2.6 8.7 %collective-permute-start = (f32[1,128]{1,0:T(1,128)}, f32[1,128]{1,0:T(1,128)S(1)}, u32[]{:S(2)}, u32[]{:S(2)}) collective-permute-start(f32[1,128]{1,0:T(1,128)} %get-tuple-element.52), channel_id=1, source_target_pairs={{0,8},{8,0},{16,24},{24,16},{32,40},{40,32},{48,56},{56,48},{64,72... | collective-permute-start | bytes 1544 | tf_op jit(solution)/shard_map/ppermute | solution.py:251
  4.5 4.5 %copy-start.20 = (f32[640]{0:T(1024)S(1)}, f32[640]{0:T(1024)}, u32[]{:S(2)}) copy-start(f32[640]{0:T(1024)} %param.11) | copy-start | bytes 7684
  4.6 6.7 %collective-permute-start.1 = (f32[1,128]{1,0:T(1,128)S(1)}, f32[1,128]{1,0:T(1,128)S(1)}, u32[]{:S(2)}, u32[]{:S(2)}) collective-permute-start(f32[1,128]{1,0:T(1,128)S(1)} %copy-done.22), channel_id=1, source_target_pairs={{0,128},{128,0},{8,136},{136,8},{16,144},{144,16},{24,152},{152,24... | collective-permute-start | bytes 1544 | tf_op jit(solution)/shard_map/ppermute | solution.py:251
  9.1 82.8 %copy-start.8 = (f32[1,640]{1,0:T(1,128)}, f32[1,640]{1,0:T(1,128)S(1)}, u32[]{:S(2)}) copy-start(f32[1,640]{1,0:T(1,128)S(1)} %broadcast_in_dim.13.kg_ref.refs_5_) | copy-start | bytes 7684
  9.1 1.0 copy-start
  10.1 1.0 copy-start.3
  11.1 21.7 %copy-start.1 = (bf16[256,640]{1,0:T(8,128)(2,1)S(1)}, bf16[256,640]{1,0:T(8,128)(2,1)}, u32[]{:S(2)}) copy-start(bf16[256,640]{1,0:T(8,128)(2,1)} %refs_6_.1) | copy-start | bytes 983044
  11.1 21.7 %copy-start.4 = (bf16[256,640]{1,0:T(8,128)(2,1)S(1)}, bf16[256,640]{1,0:T(8,128)(2,1)}, u32[]{:S(2)}) copy-start(bf16[256,640]{1,0:T(8,128)(2,1)} %refs_2_.1) | copy-start | bytes 983044
  32.2 0.5 copy-start.10
  32.7 1.0 copy-start.6
  33.7 58.1 %copy-start.7 = (bf16[256,640]{1,0:T(8,128)(2,1)S(1)}, bf16[256,640]{1,0:T(8,128)(2,1)}, u32[]{:S(2)}) copy-start(bf16[256,640]{1,0:T(8,128)(2,1)} %v_ref.3) | copy-start | bytes 983044
  33.7 58.1 %copy-start.12 = (bf16[256,640]{1,0:T(8,128)(2,1)S(1)}, bf16[256,640]{1,0:T(8,128)(2,1)}, u32[]{:S(2)}) copy-start(bf16[256,640]{1,0:T(8,128)(2,1)} %do_ref.1) | copy-start | bytes 983044
  34.9 25.7 %collective-permute-start.2 = (bf16[2,128,640]{2,1,0:T(8,128)(2,1)S(1)}, bf16[2,128,640]{2,1,0:T(8,128)(2,1)S(1)}, u32[]{:S(2)}, u32[]{:S(2)}) collective-permute-start(bf16[2,128,640]{2,1,0:T(8,128)(2,1)S(1)} %get-tuple-element.57), channel_id=1, source_target_pairs={{0,128},{128,0},{8,136},{136,8},{16,144},{144,16},{24,152},{152,24... | collective-permute-start | bytes 983048 | tf_op jit(solution)/shard_map/ppermute | solution.py:33
  40.6 21.9 %collective-permute-start.3 = (bf16[2,128,640]{2,1,0:T(8,128)(2,1)S(1)}, bf16[2,128,640]{2,1,0:T(8,128)(2,1)S(1)}, u32[]{:S(2)}, u32[]{:S(2)}) collective-permute-start(bf16[2,128,640]{2,1,0:T(8,128)(2,1)S(1)} %get-tuple-element.60), channel_id=1, source_target_pairs={{128,256},{256,128},{136,264},{264,136},{144,272},{272,144},{152,2... | collective-permute-start | bytes 983048 | tf_op jit(solution)/shard_map/ppermute | solution.py:33
  41.3 32.3 %collective-permute-start.4 = (bf16[2,128,640]{2,1,0:T(8,128)(2,1)S(1)}, bf16[2,128,640]{2,1,0:T(8,128)(2,1)S(1)}, u32[]{:S(2)}, u32[]{:S(2)}) collective-permute-start(bf16[2,128,640]{2,1,0:T(8,128)(2,1)S(1)} %get-tuple-element.63), channel_id=1, source_target_pairs={{0,256},{256,0},{8,264},{264,8},{16,272},{272,16},{24,280},{280,24... | collective-permute-start | bytes 983048 | tf_op jit(solution)/shard_map/ppermute | solution.py:33
  48.0 29.1 %collective-permute-start.5 = (bf16[2,128,640]{2,1,0:T(8,128)(2,1)S(1)}, bf16[2,128,640]{2,1,0:T(8,128)(2,1)S(1)}, u32[]{:S(2)}, u32[]{:S(2)}) collective-permute-start(bf16[2,128,640]{2,1,0:T(8,128)(2,1)S(1)} %get-tuple-element.66), channel_id=1, source_target_pairs={{0,32},{32,0},{8,40},{40,8},{16,48},{48,16},{24,56},{56,24},{64,96... | collective-permute-start | bytes 983048 | tf_op jit(solution)/shard_map/ppermute | solution.py:33
  52.9 26.1 %collective-permute-start.6 = (bf16[2,128,640]{2,1,0:T(8,128)(2,1)S(1)}, bf16[2,128,640]{2,1,0:T(8,128)(2,1)S(1)}, u32[]{:S(2)}, u32[]{:S(2)}) collective-permute-start(bf16[2,128,640]{2,1,0:T(8,128)(2,1)S(1)} %get-tuple-element.69), channel_id=1, source_target_pairs={{32,64},{64,32},{40,72},{72,40},{48,80},{80,48},{56,88},{88,56},{9... | collective-permute-start | bytes 983048 | tf_op jit(solution)/shard_map/ppermute | solution.py:33
  60.6 20.4 %collective-permute-start.7 = (bf16[2,128,640]{2,1,0:T(8,128)(2,1)S(1)}, bf16[2,128,640]{2,1,0:T(8,128)(2,1)S(1)}, u32[]{:S(2)}, u32[]{:S(2)}) collective-permute-start(bf16[2,128,640]{2,1,0:T(8,128)(2,1)S(1)} %get-tuple-element.72), channel_id=1, source_target_pairs={{0,64},{64,0},{8,72},{72,8},{16,80},{80,16},{24,88},{88,24},{32,96... | collective-permute-start | bytes 983048 | tf_op jit(solution)/shard_map/ppermute | solution.py:33
  62.5 24.6 %collective-permute-start.8 = (bf16[2,128,640]{2,1,0:T(8,128)(2,1)S(1)}, bf16[2,128,640]{2,1,0:T(8,128)(2,1)S(1)}, u32[]{:S(2)}, u32[]{:S(2)}) collective-permute-start(bf16[2,128,640]{2,1,0:T(8,128)(2,1)S(1)} %get-tuple-element.74), channel_id=1, source_target_pairs={{64,128},{128,64},{72,136},{136,72},{80,144},{144,80},{88,152},{15... | collective-permute-start | bytes 983048 | tf_op jit(solution)/shard_map/ppermute | solution.py:33
  73.6 13.5 %collective-permute-start.9 = (bf16[2,128,640]{2,1,0:T(8,128)(2,1)S(1)}, bf16[2,128,640]{2,1,0:T(8,128)(2,1)S(1)}, u32[]{:S(2)}, u32[]{:S(2)}) collective-permute-start(bf16[2,128,640]{2,1,0:T(8,128)(2,1)S(1)} %get-tuple-element.75), channel_id=1, source_target_pairs={{0,16},{16,0},{8,24},{24,8},{32,48},{48,32},{40,56},{56,40},{64,80... | collective-permute-start | bytes 983048 | tf_op jit(solution)/shard_map/ppermute | solution.py:33
  77.1 11.1 %collective-permute-start.10 = (bf16[2,128,640]{2,1,0:T(8,128)(2,1)S(1)}, bf16[2,128,640]{2,1,0:T(8,128)(2,1)S(1)}, u32[]{:S(2)}, u32[]{:S(2)}) collective-permute-start(bf16[2,128,640]{2,1,0:T(8,128)(2,1)S(1)} %get-tuple-element.76), channel_id=1, source_target_pairs={{16,32},{32,16},{24,40},{40,24},{48,64},{64,48},{56,72},{72,56},{8... | collective-permute-start | bytes 983048 | tf_op jit(solution)/shard_map/ppermute | solution.py:33
  79.0 9.1 %collective-permute-start.11 = (bf16[2,128,640]{2,1,0:T(8,128)(2,1)S(1)}, bf16[2,128,640]{2,1,0:T(8,128)(2,1)S(1)}, u32[]{:S(2)}, u32[]{:S(2)}) collective-permute-start(bf16[2,128,640]{2,1,0:T(8,128)(2,1)S(1)} %get-tuple-element.77), channel_id=1, source_target_pairs={{0,8},{8,0},{16,24},{24,16},{32,40},{40,32},{48,56},{56,48},{64,72... | collective-permute-start | bytes 983048 | tf_op jit(solution)/shard_map/ppermute | solution.py:33
  81.0 10.9 %collective-permute-start.12 = (bf16[2,128,640]{2,1,0:T(8,128)(2,1)S(1)}, bf16[2,128,640]{2,1,0:T(8,128)(2,1)S(1)}, u32[]{:S(2)}, u32[]{:S(2)}) collective-permute-start(bf16[2,128,640]{2,1,0:T(8,128)(2,1)S(1)} %get-tuple-element.78), channel_id=1, source_target_pairs={{8,16},{16,8},{24,32},{32,24},{40,48},{48,40},{56,64},{64,56},{72,... | collective-permute-start | bytes 983048 | tf_op jit(solution)/shard_map/ppermute | solution.py:33
  91.9 0.7 copy-start.11
  101.9 19.6 %collective-permute-start.23 = (bf16[2,128,640]{2,1,0:T(8,128)(2,1)S(1)}, bf16[2,128,640]{2,1,0:T(8,128)(2,1)S(1)}, u32[]{:S(2)}, u32[]{:S(2)}) collective-permute-start(bf16[2,128,640]{2,1,0:T(8,128)(2,1)S(1)} %get-tuple-element.89), channel_id=1, source_target_pairs={{0,256},{256,0},{8,264},{264,8},{16,272},{272,16},{24,280},{280,24... | collective-permute-start | bytes 983048 | tf_op jit(solution)/shard_map/ppermute | solution.py:33
  109.7 22.4 %collective-permute-start.14 = (bf16[2,128,640]{2,1,0:T(8,128)(2,1)S(1)}, bf16[2,128,640]{2,1,0:T(8,128)(2,1)S(1)}, u32[]{:S(2)}, u32[]{:S(2)}) collective-permute-start(bf16[2,128,640]{2,1,0:T(8,128)(2,1)S(1)} %get-tuple-element.84), channel_id=1, source_target_pairs={{8,16},{16,8},{24,32},{32,24},{40,48},{48,40},{56,64},{64,56},{72,... | collective-permute-start | bytes 983048 | tf_op jit(solution)/shard_map/ppermute | solution.py:33
  112.1 21.9 %collective-permute-start.13 = (bf16[2,128,640]{2,1,0:T(8,128)(2,1)S(1)}, bf16[2,128,640]{2,1,0:T(8,128)(2,1)S(1)}, u32[]{:S(2)}, u32[]{:S(2)}) collective-permute-start(bf16[2,128,640]{2,1,0:T(8,128)(2,1)S(1)} %get-tuple-element.84), channel_id=1, source_target_pairs={{0,8},{8,0},{16,24},{24,16},{32,40},{40,32},{48,56},{56,48},{64,72... | collective-permute-start | bytes 983048 | tf_op jit(solution)/shard_map/ppermute | solution.py:33
  114.0 25.8 %collective-permute-start.16 = (bf16[2,128,640]{2,1,0:T(8,128)(2,1)S(1)}, bf16[2,128,640]{2,1,0:T(8,128)(2,1)S(1)}, u32[]{:S(2)}, u32[]{:S(2)}) collective-permute-start(bf16[2,128,640]{2,1,0:T(8,128)(2,1)S(1)} %get-tuple-element.85), channel_id=1, source_target_pairs={{16,32},{32,16},{24,40},{40,24},{48,64},{64,48},{56,72},{72,56},{8... | collective-permute-start | bytes 983048 | tf_op jit(solution)/shard_map/ppermute | solution.py:33
  119.7 22.2 %collective-permute-start.15 = (bf16[2,128,640]{2,1,0:T(8,128)(2,1)S(1)}, bf16[2,128,640]{2,1,0:T(8,128)(2,1)S(1)}, u32[]{:S(2)}, u32[]{:S(2)}) collective-permute-start(bf16[2,128,640]{2,1,0:T(8,128)(2,1)S(1)} %get-tuple-element.85), channel_id=1, source_target_pairs={{0,16},{16,0},{8,24},{24,8},{32,48},{48,32},{40,56},{56,40},{64,80... | collective-permute-start | bytes 983048 | tf_op jit(solution)/shard_map/ppermute | solution.py:33
  121.6 60.6 %copy-start.13 = (bf16[2,128,640]{2,1,0:T(8,128)(2,1)}, bf16[2,128,640]{2,1,0:T(8,128)(2,1)S(1)}, u32[]{:S(2)}) copy-start(bf16[2,128,640]{2,1,0:T(8,128)(2,1)S(1)} %collective-permute-done.23.refs_12_) | copy-start | bytes 983044
  121.6 21.6 %collective-permute-start.18 = (bf16[2,128,640]{2,1,0:T(8,128)(2,1)S(1)}, bf16[2,128,640]{2,1,0:T(8,128)(2,1)S(1)}, u32[]{:S(2)}, u32[]{:S(2)}) collective-permute-start(bf16[2,128,640]{2,1,0:T(8,128)(2,1)S(1)} %get-tuple-element.86), channel_id=1, source_target_pairs={{32,64},{64,32},{40,72},{72,40},{48,80},{80,48},{56,88},{88,56},{9... | collective-permute-start | bytes 983048 | tf_op jit(solution)/shard_map/ppermute | solution.py:33
  132.1 50.1 %copy-start.14 = (bf16[2,128,640]{2,1,0:T(8,128)(2,1)}, bf16[2,128,640]{2,1,0:T(8,128)(2,1)S(1)}, u32[]{:S(2)}) copy-start(bf16[2,128,640]{2,1,0:T(8,128)(2,1)S(1)} %collective-permute-done.14.refs_3_) | copy-start | bytes 983044
  132.1 50.1 %collective-permute-start.17 = (bf16[2,128,640]{2,1,0:T(8,128)(2,1)S(1)}, bf16[2,128,640]{2,1,0:T(8,128)(2,1)}, u32[]{:S(2)}, u32[]{:S(2)}) collective-permute-start(bf16[2,128,640]{2,1,0:T(8,128)(2,1)S(1)} %get-tuple-element.86), channel_id=1, source_target_pairs={{0,32},{32,0},{8,40},{40,8},{16,48},{48,16},{24,56},{56,24},{64,96... | collective-permute-start | bytes 983048 | tf_op jit(solution)/shard_map/ppermute | solution.py:33
  134.0 48.2 %copy-start.15 = (bf16[2,128,640]{2,1,0:T(8,128)(2,1)}, bf16[2,128,640]{2,1,0:T(8,128)(2,1)S(1)}, u32[]{:S(2)}) copy-start(bf16[2,128,640]{2,1,0:T(8,128)(2,1)S(1)} %collective-permute-done.13.refs_2_) | copy-start | bytes 983044
  134.0 48.2 %collective-permute-start.20 = (bf16[2,128,640]{2,1,0:T(8,128)(2,1)S(1)}, bf16[2,128,640]{2,1,0:T(8,128)(2,1)}, u32[]{:S(2)}, u32[]{:S(2)}) collective-permute-start(bf16[2,128,640]{2,1,0:T(8,128)(2,1)S(1)} %get-tuple-element.87), channel_id=1, source_target_pairs={{64,128},{128,64},{72,136},{136,72},{80,144},{144,80},{88,152},{15... | collective-permute-start | bytes 983048 | tf_op jit(solution)/shard_map/ppermute | solution.py:33
  139.9 10.2 %copy-start.16 = (bf16[2,128,640]{2,1,0:T(8,128)(2,1)}, bf16[2,128,640]{2,1,0:T(8,128)(2,1)S(1)}, u32[]{:S(2)}) copy-start(bf16[2,128,640]{2,1,0:T(8,128)(2,1)S(1)} %collective-permute-done.16.refs_5_) | copy-start | bytes 983044
  139.9 42.3 %collective-permute-start.19 = (bf16[2,128,640]{2,1,0:T(8,128)(2,1)S(1)}, bf16[2,128,640]{2,1,0:T(8,128)(2,1)}, u32[]{:S(2)}, u32[]{:S(2)}) collective-permute-start(bf16[2,128,640]{2,1,0:T(8,128)(2,1)S(1)} %get-tuple-element.87), channel_id=1, source_target_pairs={{0,64},{64,0},{8,72},{72,8},{16,80},{80,16},{24,88},{88,24},{32,96... | collective-permute-start | bytes 983048 | tf_op jit(solution)/shard_map/ppermute | solution.py:33
  141.8 8.3 %copy-start.17 = (bf16[2,128,640]{2,1,0:T(8,128)(2,1)}, bf16[2,128,640]{2,1,0:T(8,128)(2,1)S(1)}, u32[]{:S(2)}) copy-start(bf16[2,128,640]{2,1,0:T(8,128)(2,1)S(1)} %collective-permute-done.15.refs_4_) | copy-start | bytes 983044
  141.8 40.4 %collective-permute-start.22 = (bf16[2,128,640]{2,1,0:T(8,128)(2,1)S(1)}, bf16[2,128,640]{2,1,0:T(8,128)(2,1)}, u32[]{:S(2)}, u32[]{:S(2)}) collective-permute-start(bf16[2,128,640]{2,1,0:T(8,128)(2,1)S(1)} %get-tuple-element.88), channel_id=1, source_target_pairs={{128,256},{256,128},{136,264},{264,136},{144,272},{272,144},{152,2... | collective-permute-start | bytes 983048 | tf_op jit(solution)/shard_map/ppermute | solution.py:33
  143.2 6.9 %copy-start.18 = (bf16[2,128,640]{2,1,0:T(8,128)(2,1)}, bf16[2,128,640]{2,1,0:T(8,128)(2,1)S(1)}, u32[]{:S(2)}) copy-start(bf16[2,128,640]{2,1,0:T(8,128)(2,1)S(1)} %collective-permute-done.18.refs_7_) | copy-start | bytes 983044
  143.2 39.0 %collective-permute-start.21 = (bf16[2,128,640]{2,1,0:T(8,128)(2,1)S(1)}, bf16[2,128,640]{2,1,0:T(8,128)(2,1)}, u32[]{:S(2)}, u32[]{:S(2)}) collective-permute-start(bf16[2,128,640]{2,1,0:T(8,128)(2,1)S(1)} %get-tuple-element.88), channel_id=1, source_target_pairs={{0,128},{128,0},{8,136},{136,8},{16,144},{144,16},{24,152},{152,24... | collective-permute-start | bytes 983048 | tf_op jit(solution)/shard_map/ppermute | solution.py:33
  182.3 20.4 %copy-start.2 = (bf16[256,640]{1,0:T(8,128)(2,1)S(1)}, bf16[256,640]{1,0:T(8,128)(2,1)}, u32[]{:S(2)}) copy-start(bf16[256,640]{1,0:T(8,128)(2,1)} %refs_6_.1) | copy-start | bytes 983044
  186.8 0.7 copy-start.21
  202.7 0.7 copy-start.9
  203.3 1.1 copy-start.5

commit v3 on v2

--- a/solution.py
+++ b/solution.py
@@ -19,7 +19,7 @@
 
 
 ORDER = ((4, 0), (4, 1), (5, 0), (2, 0), (2, 1), (3, 0), (3, 1), (1, 0), (1, 1), (0, 0), (0, 1))
-WINDOW = 5
+WINDOW = 6
 
 
 def pairs_of(way, count=64):
@@ -298,6 +298,7 @@
         far=[dk, dv, *backs],
     )
     q_inner, k_inner = lax.psum((q_inner, k_inner), "tp")
+    gains, k_inner = after(gains, k_inner)
     dq_pre, dk_pre = call(
         functools.partial(back_kernel, width),
         [struct((rows, cols), bf16)] * 2,

time: 207 us -> 207 us (level)
  no operation moved by 1% of the time
where the time goes in v3:
time: 207 us; the launch traced here: 206 us
  starting transfers between devices  94.2 us (46%)
  blocking collectives  67.6 us (33%)
  Pallas kernels  17.7 us (9%)
  waiting for transfers between devices  17.1 us (8%)
  local copies, waits for them, and re-layouts  7.19 us (3%)
    ppermute x22, starting transfers between devices, move(): return lax.ppermute(value, CTX, pairs_of(way))  87.8 us
    psum x2, blocking collectives, per_device(): gains = lax.psum(lax.psum(gains, 'cx'), 'cy')  31.5 us
    psum x1, blocking collectives, per_device(): squares, notes = lax.psum((squares, notes), 'tp')  20.9 us
    ppermute x22, waiting for transfers between devices, move(): return lax.ppermute(value, CTX, pairs_of(way))  17.1 us
    pallas_call x5, Pallas kernels, call(): pl.pallas_call(kernel, out_shape=outs, in_specs=[SMEM] * len(scalars) + [...  16.3 us
    psum x1, blocking collectives, per_device(): q_inner, k_inner = lax.psum((q_inner, k_inner), 'tp')  15.3 us
    unnamed x46, local copies, waits for them, and re-layouts  6.57 us
    ppermute x2, starting transfers between devices, per_device(): got = lax.ppermute(code, (*CTX, 'tp'), pairs)  6.42 us
  transfers between devices with their start and end apart: 24, of which 4 were waited for; matrix products, arithmetic and copies ran while one was open for 0% of the time, Pallas kernels for 0%

profile of v3, /device:TPU:8, one launch (start us, length us, event | category | flops | bytes accessed | tf_op | source)
XLA Modules:
  0.0 205.6 jit_solution(14430396304313945680)
XLA Ops:
  0.6 0.6 pad_add_fusion.place
  1.2 1.4 notes.1
  2.6 0.0 copy-start.22
  2.6 1.9 collective-permute-start
  4.5 0.0 copy-start.20
  4.6 4.5 %collective-permute-start.1 = (f32[1,128]{1,0:T(1,128)S(1)}, f32[1,128]{1,0:T(1,128)S(1)}, u32[]{:S(2)}, u32[]{:S(2)}) collective-permute-start(f32[1,128]{1,0:T(1,128)S(1)} %copy-done.22), channel_id=1, source_target_pairs={{0,128},{128,0},{8,136},{136,8},{16,144},{144,16},{24,152},{152,24... | collective-permute-start | bytes 1544 | tf_op jit(solution)/shard_map/ppermute | solution.py:251
  9.1 0.0 copy-start
  9.1 1.0 copy-done
  10.1 1.0 copy-done.3
  11.1 0.2 square.1
  11.3 0.0 collective-permute-done
  11.3 20.9 %all-reduce.1 = (f32[1,512]{1,0:T(1,128)S(1)}, f32[1,128]{1,0:T(1,128)S(1)}) all-reduce(f32[1,512]{1,0:T(1,128)S(1)} %square.1, f32[1,128]{1,0:T(1,128)S(1)} %fusion), channel_id=1, replica_groups=mesh['cy'=8,'cx'=8,'tp'=8] {'tp'}, use_global_device_ids=true, to_apply=%region_0.1 | all-reduce | flops 640 | bytes 5120 | tf_op jit(solution)/shard_map/psum | solution.py:254
  32.2 0.5 copy-done.10
  32.7 1.0 copy-done.6
  33.7 1.1 norm.1
  34.9 5.7 %collective-permute-start.2 = (bf16[2,128,640]{2,1,0:T(8,128)(2,1)S(1)}, bf16[2,128,640]{2,1,0:T(8,128)(2,1)S(1)}, u32[]{:S(2)}, u32[]{:S(2)}) collective-permute-start(bf16[2,128,640]{2,1,0:T(8,128)(2,1)S(1)} %get-tuple-element.57), channel_id=1, source_target_pairs={{0,128},{128,0},{8,136},{136,8},{16,144},{144,16},{24,152},{152,24... | collective-permute-start | bytes 983048 | tf_op jit(solution)/shard_map/ppermute | solution.py:33
  40.6 0.7 collective-permute-start.3
  41.3 6.7 %collective-permute-start.4 = (bf16[2,128,640]{2,1,0:T(8,128)(2,1)S(1)}, bf16[2,128,640]{2,1,0:T(8,128)(2,1)S(1)}, u32[]{:S(2)}, u32[]{:S(2)}) collective-permute-start(bf16[2,128,640]{2,1,0:T(8,128)(2,1)S(1)} %get-tuple-element.63), channel_id=1, source_target_pairs={{0,256},{256,0},{8,264},{264,8},{16,272},{272,16},{24,280},{280,24... | collective-permute-start | bytes 983048 | tf_op jit(solution)/shard_map/ppermute | solution.py:33
  48.0 4.9 %collective-permute-start.5 = (bf16[2,128,640]{2,1,0:T(8,128)(2,1)S(1)}, bf16[2,128,640]{2,1,0:T(8,128)(2,1)S(1)}, u32[]{:S(2)}, u32[]{:S(2)}) collective-permute-start(bf16[2,128,640]{2,1,0:T(8,128)(2,1)S(1)} %get-tuple-element.66), channel_id=1, source_target_pairs={{0,32},{32,0},{8,40},{40,8},{16,48},{48,16},{24,56},{56,24},{64,96... | collective-permute-start | bytes 983048 | tf_op jit(solution)/shard_map/ppermute | solution.py:33
  52.9 1.9 collective-permute-start.6
  54.9 5.7 %collective-permute-done.2.refs_0_ = bf16[2,128,640]{2,1,0:T(8,128)(2,1)S(1)} collective-permute-done((bf16[2,128,640]{2,1,0:T(8,128)(2,1)S(1)}, bf16[2,128,640]{2,1,0:T(8,128)(2,1)S(1)}, u32[]{:S(2)}, u32[]{:S(2)}) %collective-permute-start.2) | collective-permute-done | bytes 327712 | tf_op jit(solution)/shard_map/ppermute | solution.py:33
  60.6 1.9 collective-permute-start.7
  62.5 0.0 collective-permute-done.3.refs_1_
  62.5 11.1 %collective-permute-start.8 = (bf16[2,128,640]{2,1,0:T(8,128)(2,1)S(1)}, bf16[2,128,640]{2,1,0:T(8,128)(2,1)S(1)}, u32[]{:S(2)}, u32[]{:S(2)}) collective-permute-start(bf16[2,128,640]{2,1,0:T(8,128)(2,1)S(1)} %get-tuple-element.72), channel_id=1, source_target_pairs={{64,128},{128,64},{72,136},{136,72},{80,144},{144,80},{88,152},{15... | collective-permute-start | bytes 983048 | tf_op jit(solution)/shard_map/ppermute | solution.py:33
  73.6 0.0 collective-permute-done.4.refs_2_
  73.6 3.5 %collective-permute-start.9 = (bf16[2,128,640]{2,1,0:T(8,128)(2,1)S(1)}, bf16[2,128,640]{2,1,0:T(8,128)(2,1)S(1)}, u32[]{:S(2)}, u32[]{:S(2)}) collective-permute-start(bf16[2,128,640]{2,1,0:T(8,128)(2,1)S(1)} %get-tuple-element.73), channel_id=1, source_target_pairs={{0,16},{16,0},{8,24},{24,8},{32,48},{48,32},{40,56},{56,40},{64,80... | collective-permute-start | bytes 983048 | tf_op jit(solution)/shard_map/ppermute | solution.py:33
  77.1 1.9 collective-permute-start.10
  79.0 0.0 collective-permute-done.6.refs_4_
  79.0 1.9 collective-permute-start.11
  81.0 6.1 %collective-permute-start.12 = (bf16[2,128,640]{2,1,0:T(8,128)(2,1)S(1)}, bf16[2,128,640]{2,1,0:T(8,128)(2,1)S(1)}, u32[]{:S(2)}, u32[]{:S(2)}) collective-permute-start(bf16[2,128,640]{2,1,0:T(8,128)(2,1)S(1)} %get-tuple-element.76), channel_id=1, source_target_pairs={{8,16},{16,8},{24,32},{32,24},{40,48},{48,40},{56,64},{64,56},{72,... | collective-permute-start | bytes 983048 | tf_op jit(solution)/shard_map/ppermute | solution.py:33
  87.1 0.0 collective-permute-done.8.refs_6_
  87.1 0.0 collective-permute-done.9.refs_7_
  87.1 1.0 collective-permute-done.10.refs_8_
  88.2 0.0 collective-permute-done.11.refs_9_
  88.2 3.7 %collective-permute-done.12.refs_10_ = bf16[2,128,640]{2,1,0:T(8,128)(2,1)S(1)} collective-permute-done((bf16[2,128,640]{2,1,0:T(8,128)(2,1)S(1)}, bf16[2,128,640]{2,1,0:T(8,128)(2,1)S(1)}, u32[]{:S(2)}, u32[]{:S(2)}) %collective-permute-start.12) | collective-permute-done | bytes 327712 | tf_op jit(solution)/shard_map/ppermute | solution.py:33
  91.9 0.6 copy-done.11
  92.5 9.4 %attention.1 = (bf16[256,640]{1,0:T(8,128)(2,1)}, f32[256,640]{1,0:T(8,128)S(1)}, f32[256,640]{1,0:T(8,128)}, f32[256,640]{1,0:T(8,128)}, f32[1,256]{1,0:T(1,128...) custom-call(s32[16]{0:T(128)S(1)} %copy-done.11, ...), custom_call_target="tpu_custom_call" | custom-call | flops 2013265920 | bytes 9516032 | tf_op jit(solution)/shard_map/attention/pallas_call | solution.py:218
  101.9 7.7 %collective-permute-start.23 = (bf16[2,128,640]{2,1,0:T(8,128)(2,1)S(1)}, bf16[2,128,640]{2,1,0:T(8,128)(2,1)S(1)}, u32[]{:S(2)}, u32[]{:S(2)}) collective-permute-start(bf16[2,128,640]{2,1,0:T(8,128)(2,1)S(1)} %get-tuple-element.88), channel_id=1, source_target_pairs={{0,256},{256,0},{8,264},{264,8},{16,272},{272,16},{24,280},{280,24... | collective-permute-start | bytes 983048 | tf_op jit(solution)/shard_map/ppermute | solution.py:33
  109.6 2.4 %collective-permute-start.14 = (bf16[2,128,640]{2,1,0:T(8,128)(2,1)S(1)}, bf16[2,128,640]{2,1,0:T(8,128)(2,1)S(1)}, u32[]{:S(2)}, u32[]{:S(2)}) collective-permute-start(bf16[2,128,640]{2,1,0:T(8,128)(2,1)S(1)} %get-tuple-element.83), channel_id=1, source_target_pairs={{8,16},{16,8},{24,32},{32,24},{40,48},{48,40},{56,64},{64,56},{72,... | collective-permute-start | bytes 983048 | tf_op jit(solution)/shard_map/ppermute | solution.py:33
  112.1 1.9 collective-permute-start.13
  114.0 5.6 %collective-permute-start.16 = (bf16[2,128,640]{2,1,0:T(8,128)(2,1)S(1)}, bf16[2,128,640]{2,1,0:T(8,128)(2,1)S(1)}, u32[]{:S(2)}, u32[]{:S(2)}) collective-permute-start(bf16[2,128,640]{2,1,0:T(8,128)(2,1)S(1)} %get-tuple-element.84), channel_id=1, source_target_pairs={{16,32},{32,16},{24,40},{40,24},{48,64},{64,48},{56,72},{72,56},{8... | collective-permute-start | bytes 983048 | tf_op jit(solution)/shard_map/ppermute | solution.py:33
  119.6 1.9 collective-permute-start.15
  121.6 3.8 %collective-permute-start.18 = (bf16[2,128,640]{2,1,0:T(8,128)(2,1)S(1)}, bf16[2,128,640]{2,1,0:T(8,128)(2,1)S(1)}, u32[]{:S(2)}, u32[]{:S(2)}) collective-permute-start(bf16[2,128,640]{2,1,0:T(8,128)(2,1)S(1)} %get-tuple-element.85), channel_id=1, source_target_pairs={{32,64},{64,32},{40,72},{72,40},{48,80},{80,48},{56,88},{88,56},{9... | collective-permute-start | bytes 983048 | tf_op jit(solution)/shard_map/ppermute | solution.py:33
  125.4 6.6 %collective-permute-done.14.refs_3_ = bf16[2,128,640]{2,1,0:T(8,128)(2,1)S(1)} collective-permute-done((bf16[2,128,640]{2,1,0:T(8,128)(2,1)S(1)}, bf16[2,128,640]{2,1,0:T(8,128)(2,1)S(1)}, u32[]{:S(2)}, u32[]{:S(2)}) %collective-permute-start.14) | collective-permute-done | bytes 327712 | tf_op jit(solution)/shard_map/ppermute | solution.py:33
  131.9 1.9 collective-permute-start.17
  133.9 0.0 collective-permute-done.13.refs_2_
  133.9 0.0 copy-start.15
  133.9 5.8 %collective-permute-start.20 = (bf16[2,128,640]{2,1,0:T(8,128)(2,1)S(1)}, bf16[2,128,640]{2,1,0:T(8,128)(2,1)}, u32[]{:S(2)}, u32[]{:S(2)}) collective-permute-start(bf16[2,128,640]{2,1,0:T(8,128)(2,1)S(1)} %get-tuple-element.86), channel_id=1, source_target_pairs={{64,128},{128,64},{72,136},{136,72},{80,144},{144,80},{88,152},{15... | collective-permute-start | bytes 983048 | tf_op jit(solution)/shard_map/ppermute | solution.py:33
  139.7 0.0 collective-permute-done.16.refs_5_
  139.7 1.9 collective-permute-start.19
  141.7 0.0 collective-permute-done.15.refs_4_
  141.7 1.4 collective-permute-start.22
  143.1 7.0 %collective-permute-start.21 = (bf16[2,128,640]{2,1,0:T(8,128)(2,1)S(1)}, bf16[2,128,640]{2,1,0:T(8,128)(2,1)}, u32[]{:S(2)}, u32[]{:S(2)}) collective-permute-start(bf16[2,128,640]{2,1,0:T(8,128)(2,1)S(1)} %get-tuple-element.87), channel_id=1, source_target_pairs={{0,128},{128,0},{8,136},{136,8},{16,144},{144,16},{24,152},{152,24... | collective-permute-start | bytes 983048 | tf_op jit(solution)/shard_map/ppermute | solution.py:33
  150.1 15.5 %psum.45 = f32[2,640]{1,0:T(2,128)S(1)} all-reduce(f32[2,640]{1,0:T(2,128)S(1)} %get-tuple-element.80), channel_id=1, replica_groups=mesh['cy'=8,'cx'=8,'tp'=8] {'cx'}, use_global_device_ids=true, to_apply=%region_3.4 | all-reduce | flops 1280 | bytes 10240 | tf_op jit(solution)/shard_map/psum | solution.py:285
  165.6 16.0 %psum.46 = f32[2,640]{1,0:T(2,128)S(1)} all-reduce(f32[2,640]{1,0:T(2,128)S(1)} %psum.45), channel_id=1, replica_groups=mesh['cy'=8,'cx'=8,'tp'=8] {'cy'}, use_global_device_ids=true, to_apply=%region_4.5 | all-reduce | flops 1280 | bytes 10240 | tf_op jit(solution)/shard_map/psum | solution.py:285
  181.6 0.0 copy-start.2
  181.7 4.5 %collect.1 = (f32[256,640]{1,0:T(8,128)}, bf16[256,640]{1,0:T(8,128)(2,1)}, f32[1,256]{1,0:T(1,128)}) custom-call(s32[16]{0:T(128)} %get-tuple-element.51.mine, s32[128]{0:T(128)} %copy-done.10, f32[1,640]{1,0:T(1,128)} %copy-done.8, bf16[256,640]{1,0:T(8,128)(2,1)} %refs_6_.1, f32[256,640]{1,0:T(8,128)} %get-tuple-element.81.refs_0_, ...), custom_call_target="tpu_custom_call" | custom-call | bytes 6229504 | tf_op jit(solution)/shard_map/collect/pallas_call | solution.py:218
  186.2 0.0 copy-start.21
  186.2 0.7 copy-done.21
  186.9 15.3 %all-reduce = (f32[1,256]{1,0:T(1,128)S(1)}, f32[1,256]{1,0:T(1,128)S(1)}) all-reduce(f32[1,256]{1,0:T(1,128)S(1)} %get-tuple-element.78, f32[1,256]{1,0:T(1,128)S(1)} %copy-done.21), channel_id=1, replica_groups=mesh['cy'=8,'cx'=8,'tp'=8] {'tp'}, use_global_device_ids=true, to_apply=%region_2.3 | all-reduce | flops 512 | bytes 4096 | tf_op jit(solution)/shard_map/psum | solution.py:300
  202.1 0.6 slice_reduce_fusion
  202.7 0.7 copy-done.9
  203.4 1.1 copy-done.5
  204.5 1.1 back.1
  (46 shorter events, 0.1 us)
Async XLA Ops:
  1.2 7.8 %copy-start.19 = (f32[640]{0:T(1024)S(1)}, f32[640]{0:T(1024)}, u32[]{:S(2)}) copy-start(f32[640]{0:T(1024)} %param.12) | copy-start | bytes 7684
  2.6 1.9 copy-start.22
  2.6 8.7 %collective-permute-start = (f32[1,128]{1,0:T(1,128)}, f32[1,128]{1,0:T(1,128)S(1)}, u32[]{:S(2)}, u32[]{:S(2)}) collective-permute-start(f32[1,128]{1,0:T(1,128)} %get-tuple-element.52), channel_id=1, source_target_pairs={{0,8},{8,0},{16,24},{24,16},{32,40},{40,32},{48,56},{56,48},{64,72... | collective-permute-start | bytes 1544 | tf_op jit(solution)/shard_map/ppermute | solution.py:251
  4.5 4.5 %copy-start.20 = (f32[640]{0:T(1024)S(1)}, f32[640]{0:T(1024)}, u32[]{:S(2)}) copy-start(f32[640]{0:T(1024)} %param.11) | copy-start | bytes 7684
  4.6 6.7 %collective-permute-start.1 = (f32[1,128]{1,0:T(1,128)S(1)}, f32[1,128]{1,0:T(1,128)S(1)}, u32[]{:S(2)}, u32[]{:S(2)}) collective-permute-start(f32[1,128]{1,0:T(1,128)S(1)} %copy-done.22), channel_id=1, source_target_pairs={{0,128},{128,0},{8,136},{136,8},{16,144},{144,16},{24,152},{152,24... | collective-permute-start | bytes 1544 | tf_op jit(solution)/shard_map/ppermute | solution.py:251
  9.1 82.8 %copy-start.8 = (f32[1,640]{1,0:T(1,128)}, f32[1,640]{1,0:T(1,128)S(1)}, u32[]{:S(2)}) copy-start(f32[1,640]{1,0:T(1,128)S(1)} %broadcast_in_dim.13.kg_ref.refs_5_) | copy-start | bytes 7684
  9.1 1.0 copy-start
  10.1 1.0 copy-start.3
  11.1 21.7 %copy-start.1 = (bf16[256,640]{1,0:T(8,128)(2,1)S(1)}, bf16[256,640]{1,0:T(8,128)(2,1)}, u32[]{:S(2)}) copy-start(bf16[256,640]{1,0:T(8,128)(2,1)} %refs_6_.1) | copy-start | bytes 983044
  11.1 21.7 %copy-start.4 = (bf16[256,640]{1,0:T(8,128)(2,1)S(1)}, bf16[256,640]{1,0:T(8,128)(2,1)}, u32[]{:S(2)}) copy-start(bf16[256,640]{1,0:T(8,128)(2,1)} %refs_2_.1) | copy-start | bytes 983044
  32.2 0.5 copy-start.10
  32.7 1.0 copy-start.6
  33.7 58.1 %copy-start.7 = (bf16[256,640]{1,0:T(8,128)(2,1)S(1)}, bf16[256,640]{1,0:T(8,128)(2,1)}, u32[]{:S(2)}) copy-start(bf16[256,640]{1,0:T(8,128)(2,1)} %v_ref.3) | copy-start | bytes 983044
  33.7 58.1 %copy-start.12 = (bf16[256,640]{1,0:T(8,128)(2,1)S(1)}, bf16[256,640]{1,0:T(8,128)(2,1)}, u32[]{:S(2)}) copy-start(bf16[256,640]{1,0:T(8,128)(2,1)} %do_ref.1) | copy-start | bytes 983044
  34.9 25.7 %collective-permute-start.2 = (bf16[2,128,640]{2,1,0:T(8,128)(2,1)S(1)}, bf16[2,128,640]{2,1,0:T(8,128)(2,1)S(1)}, u32[]{:S(2)}, u32[]{:S(2)}) collective-permute-start(bf16[2,128,640]{2,1,0:T(8,128)(2,1)S(1)} %get-tuple-element.57), channel_id=1, source_target_pairs={{0,128},{128,0},{8,136},{136,8},{16,144},{144,16},{24,152},{152,24... | collective-permute-start | bytes 983048 | tf_op jit(solution)/shard_map/ppermute | solution.py:33
  40.6 21.9 %collective-permute-start.3 = (bf16[2,128,640]{2,1,0:T(8,128)(2,1)S(1)}, bf16[2,128,640]{2,1,0:T(8,128)(2,1)S(1)}, u32[]{:S(2)}, u32[]{:S(2)}) collective-permute-start(bf16[2,128,640]{2,1,0:T(8,128)(2,1)S(1)} %get-tuple-element.60), channel_id=1, source_target_pairs={{128,256},{256,128},{136,264},{264,136},{144,272},{272,144},{152,2... | collective-permute-start | bytes 983048 | tf_op jit(solution)/shard_map/ppermute | solution.py:33
  41.3 32.3 %collective-permute-start.4 = (bf16[2,128,640]{2,1,0:T(8,128)(2,1)S(1)}, bf16[2,128,640]{2,1,0:T(8,128)(2,1)S(1)}, u32[]{:S(2)}, u32[]{:S(2)}) collective-permute-start(bf16[2,128,640]{2,1,0:T(8,128)(2,1)S(1)} %get-tuple-element.63), channel_id=1, source_target_pairs={{0,256},{256,0},{8,264},{264,8},{16,272},{272,16},{24,280},{280,24... | collective-permute-start | bytes 983048 | tf_op jit(solution)/shard_map/ppermute | solution.py:33
  48.0 29.1 %collective-permute-start.5 = (bf16[2,128,640]{2,1,0:T(8,128)(2,1)S(1)}, bf16[2,128,640]{2,1,0:T(8,128)(2,1)S(1)}, u32[]{:S(2)}, u32[]{:S(2)}) collective-permute-start(bf16[2,128,640]{2,1,0:T(8,128)(2,1)S(1)} %get-tuple-element.66), channel_id=1, source_target_pairs={{0,32},{32,0},{8,40},{40,8},{16,48},{48,16},{24,56},{56,24},{64,96... | collective-permute-start | bytes 983048 | tf_op jit(solution)/shard_map/ppermute | solution.py:33
  52.9 26.1 %collective-permute-start.6 = (bf16[2,128,640]{2,1,0:T(8,128)(2,1)S(1)}, bf16[2,128,640]{2,1,0:T(8,128)(2,1)S(1)}, u32[]{:S(2)}, u32[]{:S(2)}) collective-permute-start(bf16[2,128,640]{2,1,0:T(8,128)(2,1)S(1)} %get-tuple-element.69), channel_id=1, source_target_pairs={{32,64},{64,32},{40,72},{72,40},{48,80},{80,48},{56,88},{88,56},{9... | collective-permute-start | bytes 983048 | tf_op jit(solution)/shard_map/ppermute | solution.py:33
  60.6 20.4 %collective-permute-start.7 = (bf16[2,128,640]{2,1,0:T(8,128)(2,1)S(1)}, bf16[2,128,640]{2,1,0:T(8,128)(2,1)S(1)}, u32[]{:S(2)}, u32[]{:S(2)}) collective-permute-start(bf16[2,128,640]{2,1,0:T(8,128)(2,1)S(1)} %get-tuple-element.71), channel_id=1, source_target_pairs={{0,64},{64,0},{8,72},{72,8},{16,80},{80,16},{24,88},{88,24},{32,96... | collective-permute-start | bytes 983048 | tf_op jit(solution)/shard_map/ppermute | solution.py:33
  62.5 24.6 %collective-permute-start.8 = (bf16[2,128,640]{2,1,0:T(8,128)(2,1)S(1)}, bf16[2,128,640]{2,1,0:T(8,128)(2,1)S(1)}, u32[]{:S(2)}, u32[]{:S(2)}) collective-permute-start(bf16[2,128,640]{2,1,0:T(8,128)(2,1)S(1)} %get-tuple-element.72), channel_id=1, source_target_pairs={{64,128},{128,64},{72,136},{136,72},{80,144},{144,80},{88,152},{15... | collective-permute-start | bytes 983048 | tf_op jit(solution)/shard_map/ppermute | solution.py:33
  73.6 13.5 %collective-permute-start.9 = (bf16[2,128,640]{2,1,0:T(8,128)(2,1)S(1)}, bf16[2,128,640]{2,1,0:T(8,128)(2,1)S(1)}, u32[]{:S(2)}, u32[]{:S(2)}) collective-permute-start(bf16[2,128,640]{2,1,0:T(8,128)(2,1)S(1)} %get-tuple-element.73), channel_id=1, source_target_pairs={{0,16},{16,0},{8,24},{24,8},{32,48},{48,32},{40,56},{56,40},{64,80... | collective-permute-start | bytes 983048 | tf_op jit(solution)/shard_map/ppermute | solution.py:33
  77.1 11.1 %collective-permute-start.10 = (bf16[2,128,640]{2,1,0:T(8,128)(2,1)S(1)}, bf16[2,128,640]{2,1,0:T(8,128)(2,1)S(1)}, u32[]{:S(2)}, u32[]{:S(2)}) collective-permute-start(bf16[2,128,640]{2,1,0:T(8,128)(2,1)S(1)} %get-tuple-element.74), channel_id=1, source_target_pairs={{16,32},{32,16},{24,40},{40,24},{48,64},{64,48},{56,72},{72,56},{8... | collective-permute-start | bytes 983048 | tf_op jit(solution)/shard_map/ppermute | solution.py:33
  79.0 9.1 %collective-permute-start.11 = (bf16[2,128,640]{2,1,0:T(8,128)(2,1)S(1)}, bf16[2,128,640]{2,1,0:T(8,128)(2,1)S(1)}, u32[]{:S(2)}, u32[]{:S(2)}) collective-permute-start(bf16[2,128,640]{2,1,0:T(8,128)(2,1)S(1)} %get-tuple-element.75), channel_id=1, source_target_pairs={{0,8},{8,0},{16,24},{24,16},{32,40},{40,32},{48,56},{56,48},{64,72... | collective-permute-start | bytes 983048 | tf_op jit(solution)/shard_map/ppermute | solution.py:33
  81.0 10.9 %collective-permute-start.12 = (bf16[2,128,640]{2,1,0:T(8,128)(2,1)S(1)}, bf16[2,128,640]{2,1,0:T(8,128)(2,1)S(1)}, u32[]{:S(2)}, u32[]{:S(2)}) collective-permute-start(bf16[2,128,640]{2,1,0:T(8,128)(2,1)S(1)} %get-tuple-element.76), channel_id=1, source_target_pairs={{8,16},{16,8},{24,32},{32,24},{40,48},{48,40},{56,64},{64,56},{72,... | collective-permute-start | bytes 983048 | tf_op jit(solution)/shard_map/ppermute | solution.py:33
  91.9 0.7 copy-start.11
  101.9 19.6 %collective-permute-start.23 = (bf16[2,128,640]{2,1,0:T(8,128)(2,1)S(1)}, bf16[2,128,640]{2,1,0:T(8,128)(2,1)S(1)}, u32[]{:S(2)}, u32[]{:S(2)}) collective-permute-start(bf16[2,128,640]{2,1,0:T(8,128)(2,1)S(1)} %get-tuple-element.88), channel_id=1, source_target_pairs={{0,256},{256,0},{8,264},{264,8},{16,272},{272,16},{24,280},{280,24... | collective-permute-start | bytes 983048 | tf_op jit(solution)/shard_map/ppermute | solution.py:33
  109.6 22.3 %collective-permute-start.14 = (bf16[2,128,640]{2,1,0:T(8,128)(2,1)S(1)}, bf16[2,128,640]{2,1,0:T(8,128)(2,1)S(1)}, u32[]{:S(2)}, u32[]{:S(2)}) collective-permute-start(bf16[2,128,640]{2,1,0:T(8,128)(2,1)S(1)} %get-tuple-element.83), channel_id=1, source_target_pairs={{8,16},{16,8},{24,32},{32,24},{40,48},{48,40},{56,64},{64,56},{72,... | collective-permute-start | bytes 983048 | tf_op jit(solution)/shard_map/ppermute | solution.py:33
  112.1 21.8 %collective-permute-start.13 = (bf16[2,128,640]{2,1,0:T(8,128)(2,1)S(1)}, bf16[2,128,640]{2,1,0:T(8,128)(2,1)S(1)}, u32[]{:S(2)}, u32[]{:S(2)}) collective-permute-start(bf16[2,128,640]{2,1,0:T(8,128)(2,1)S(1)} %get-tuple-element.83), channel_id=1, source_target_pairs={{0,8},{8,0},{16,24},{24,16},{32,40},{40,32},{48,56},{56,48},{64,72... | collective-permute-start | bytes 983048 | tf_op jit(solution)/shard_map/ppermute | solution.py:33
  114.0 25.7 %collective-permute-start.16 = (bf16[2,128,640]{2,1,0:T(8,128)(2,1)S(1)}, bf16[2,128,640]{2,1,0:T(8,128)(2,1)S(1)}, u32[]{:S(2)}, u32[]{:S(2)}) collective-permute-start(bf16[2,128,640]{2,1,0:T(8,128)(2,1)S(1)} %get-tuple-element.84), channel_id=1, source_target_pairs={{16,32},{32,16},{24,40},{40,24},{48,64},{64,48},{56,72},{72,56},{8... | collective-permute-start | bytes 983048 | tf_op jit(solution)/shard_map/ppermute | solution.py:33
  119.6 22.0 %collective-permute-start.15 = (bf16[2,128,640]{2,1,0:T(8,128)(2,1)S(1)}, bf16[2,128,640]{2,1,0:T(8,128)(2,1)S(1)}, u32[]{:S(2)}, u32[]{:S(2)}) collective-permute-start(bf16[2,128,640]{2,1,0:T(8,128)(2,1)S(1)} %get-tuple-element.84), channel_id=1, source_target_pairs={{0,16},{16,0},{8,24},{24,8},{32,48},{48,32},{40,56},{56,40},{64,80... | collective-permute-start | bytes 983048 | tf_op jit(solution)/shard_map/ppermute | solution.py:33
  121.6 60.0 %copy-start.13 = (bf16[2,128,640]{2,1,0:T(8,128)(2,1)}, bf16[2,128,640]{2,1,0:T(8,128)(2,1)S(1)}, u32[]{:S(2)}) copy-start(bf16[2,128,640]{2,1,0:T(8,128)(2,1)S(1)} %collective-permute-done.23.refs_12_) | copy-start | bytes 983044
  121.6 21.5 %collective-permute-start.18 = (bf16[2,128,640]{2,1,0:T(8,128)(2,1)S(1)}, bf16[2,128,640]{2,1,0:T(8,128)(2,1)S(1)}, u32[]{:S(2)}, u32[]{:S(2)}) collective-permute-start(bf16[2,128,640]{2,1,0:T(8,128)(2,1)S(1)} %get-tuple-element.85), channel_id=1, source_target_pairs={{32,64},{64,32},{40,72},{72,40},{48,80},{80,48},{56,88},{88,56},{9... | collective-permute-start | bytes 983048 | tf_op jit(solution)/shard_map/ppermute | solution.py:33
  131.9 49.7 %copy-start.14 = (bf16[2,128,640]{2,1,0:T(8,128)(2,1)}, bf16[2,128,640]{2,1,0:T(8,128)(2,1)S(1)}, u32[]{:S(2)}) copy-start(bf16[2,128,640]{2,1,0:T(8,128)(2,1)S(1)} %collective-permute-done.14.refs_3_) | copy-start | bytes 983044
  131.9 49.6 %collective-permute-start.17 = (bf16[2,128,640]{2,1,0:T(8,128)(2,1)S(1)}, bf16[2,128,640]{2,1,0:T(8,128)(2,1)}, u32[]{:S(2)}, u32[]{:S(2)}) collective-permute-start(bf16[2,128,640]{2,1,0:T(8,128)(2,1)S(1)} %get-tuple-element.85), channel_id=1, source_target_pairs={{0,32},{32,0},{8,40},{40,8},{16,48},{48,16},{24,56},{56,24},{64,96... | collective-permute-start | bytes 983048 | tf_op jit(solution)/shard_map/ppermute | solution.py:33
  133.9 47.8 %copy-start.15 = (bf16[2,128,640]{2,1,0:T(8,128)(2,1)}, bf16[2,128,640]{2,1,0:T(8,128)(2,1)S(1)}, u32[]{:S(2)}) copy-start(bf16[2,128,640]{2,1,0:T(8,128)(2,1)S(1)} %collective-permute-done.13.refs_2_) | copy-start | bytes 983044
  133.9 47.7 %collective-permute-start.20 = (bf16[2,128,640]{2,1,0:T(8,128)(2,1)S(1)}, bf16[2,128,640]{2,1,0:T(8,128)(2,1)}, u32[]{:S(2)}, u32[]{:S(2)}) collective-permute-start(bf16[2,128,640]{2,1,0:T(8,128)(2,1)S(1)} %get-tuple-element.86), channel_id=1, source_target_pairs={{64,128},{128,64},{72,136},{136,72},{80,144},{144,80},{88,152},{15... | collective-permute-start | bytes 983048 | tf_op jit(solution)/shard_map/ppermute | solution.py:33
  139.7 10.3 %copy-start.16 = (bf16[2,128,640]{2,1,0:T(8,128)(2,1)}, bf16[2,128,640]{2,1,0:T(8,128)(2,1)S(1)}, u32[]{:S(2)}) copy-start(bf16[2,128,640]{2,1,0:T(8,128)(2,1)S(1)} %collective-permute-done.16.refs_5_) | copy-start | bytes 983044
  139.7 41.9 %collective-permute-start.19 = (bf16[2,128,640]{2,1,0:T(8,128)(2,1)S(1)}, bf16[2,128,640]{2,1,0:T(8,128)(2,1)}, u32[]{:S(2)}, u32[]{:S(2)}) collective-permute-start(bf16[2,128,640]{2,1,0:T(8,128)(2,1)S(1)} %get-tuple-element.86), channel_id=1, source_target_pairs={{0,64},{64,0},{8,72},{72,8},{16,80},{80,16},{24,88},{88,24},{32,96... | collective-permute-start | bytes 983048 | tf_op jit(solution)/shard_map/ppermute | solution.py:33
  141.7 8.4 %copy-start.17 = (bf16[2,128,640]{2,1,0:T(8,128)(2,1)}, bf16[2,128,640]{2,1,0:T(8,128)(2,1)S(1)}, u32[]{:S(2)}) copy-start(bf16[2,128,640]{2,1,0:T(8,128)(2,1)S(1)} %collective-permute-done.15.refs_4_) | copy-start | bytes 983044
  141.7 39.9 %collective-permute-start.22 = (bf16[2,128,640]{2,1,0:T(8,128)(2,1)S(1)}, bf16[2,128,640]{2,1,0:T(8,128)(2,1)}, u32[]{:S(2)}, u32[]{:S(2)}) collective-permute-start(bf16[2,128,640]{2,1,0:T(8,128)(2,1)S(1)} %get-tuple-element.87), channel_id=1, source_target_pairs={{128,256},{256,128},{136,264},{264,136},{144,272},{272,144},{152,2... | collective-permute-start | bytes 983048 | tf_op jit(solution)/shard_map/ppermute | solution.py:33
  143.1 7.0 %copy-start.18 = (bf16[2,128,640]{2,1,0:T(8,128)(2,1)}, bf16[2,128,640]{2,1,0:T(8,128)(2,1)S(1)}, u32[]{:S(2)}) copy-start(bf16[2,128,640]{2,1,0:T(8,128)(2,1)S(1)} %collective-permute-done.18.refs_7_) | copy-start | bytes 983044
  143.1 38.5 %collective-permute-start.21 = (bf16[2,128,640]{2,1,0:T(8,128)(2,1)S(1)}, bf16[2,128,640]{2,1,0:T(8,128)(2,1)}, u32[]{:S(2)}, u32[]{:S(2)}) collective-permute-start(bf16[2,128,640]{2,1,0:T(8,128)(2,1)S(1)} %get-tuple-element.87), channel_id=1, source_target_pairs={{0,128},{128,0},{8,136},{136,8},{16,144},{144,16},{24,152},{152,24... | collective-permute-start | bytes 983048 | tf_op jit(solution)/shard_map/ppermute | solution.py:33
  181.6 21.1 %copy-start.2 = (bf16[256,640]{1,0:T(8,128)(2,1)S(1)}, bf16[256,640]{1,0:T(8,128)(2,1)}, u32[]{:S(2)}) copy-start(bf16[256,640]{1,0:T(8,128)(2,1)} %refs_6_.1) | copy-start | bytes 983044
  186.2 0.7 copy-start.21
  202.7 0.7 copy-start.9
  203.4 1.1 copy-start.5
